TPU v7x, 32 devices: a whole 2x2x4 slice. The times are simulated.
32 devices in a mesh: row: 8 (over z, core), col: 4 (over y, x).
Axes of the slice: x: 2, y: 2, z: 4, core: 2. Of those that a mesh axis runs over, the one named last changes fastest.
Arguments:
- front_entries: float32 [16384, 16384], P('row', 'col'), may hold values from 0 to 3, as said below
- tile_group: int32 [32], replicated, may hold values from 0 to 3
- child_factor: bfloat16 [16384, 256], P('row', 'col'), may hold values from -0.375 to 0.375
- row_map: int32 [128], replicated, may hold values from 0 to 127, as said below
Outputs:
- factor_panels: bfloat16 [16384, 512], P('row', 'col')
- schur_block: float32 [16384, 16384], P('row', 'col')
Inputs may be any that keep to these rules, and one draw needn't show every extreme that they name: `front_entries`: Symmetric; assembled is positive definite. `row_map`: A permutation of the parent tiles. The tile in row block r (blocks of 2048 rows) goes to a parent tile in row block r or in the row block whose index differs from r in the highest bit.
All inputs are finite; a program needn't handle non-finite values.
Results may differ from a plain program's by a relative error of at most 0.0026.
Values may be sent and summed in bfloat16 or wider, within the bound.
No kernel may reach another device: no remote copies, remote signals or barrier semaphores. Data moves between devices by JAX's collectives and lax.ppermute only.
A program may use at most 192 MiB of HBM per device.

v0:
```python
import functools

import jax
import jax.numpy as jnp
from jax import lax
from jax.experimental import pallas as pl
from jax.experimental.pallas import tpu as pltpu
from jax.sharding import PartitionSpec as P

PW = 256
NP = 2
TS = 128
MT = 512
NPIV = NP * PW
BLK = 32
F32 = jnp.float32
BF16 = jnp.bfloat16
VMEM_BYTES = 60 * 1024 * 1024

NN = (((1,), (0,)), ((), ()))
NT = (((1,), (1,)), ((), ()))


def dot(left, right, dims=NN, precision=None):
    return lax.dot_general(left, right, dims, precision=precision, preferred_element_type=F32)


def exact(left, right, dims=NN):
    return dot(left, right, dims, lax.Precision.HIGHEST)


def split(value):
    high = value.astype(BF16)
    return high, (value - high.astype(F32)).astype(BF16)


def swapped(value, axis, mask):
    if mask == 0:
        return value
    return lax.ppermute(value, axis, [(i, i ^ mask) for i in range(lax.axis_size(axis))])


def whole_spec():
    return pl.BlockSpec(memory_space=pltpu.VMEM)


def smem_spec():
    return pl.BlockSpec(memory_space=pltpu.SMEM)


def factor_diagonal(block):
    groups = BLK // 8
    lane = lax.broadcasted_iota(jnp.int32, (BLK, 128), 1)
    row = lax.broadcasted_iota(jnp.int32, (BLK, 128), 0)
    row8 = lax.broadcasted_iota(jnp.int32, (8, 128), 0)
    start = jnp.where(lane < BLK, block, jnp.where(lane == row + BLK, 1.0, 0.0))
    work = [start[8 * g : 8 * g + 8] for g in range(groups)]
    cols = []
    for k in range(BLK):
        base = 8 * (k // 8)
        cols.append(jnp.broadcast_to(block[base:, k : k + 1], (BLK - base, 128)))
    scale = [jnp.ones((8, 128), F32) for _ in range(groups)]
    for j in range(BLK):
        g0 = j // 8
        base = 8 * g0
        column = cols[j]
        pivot = column[j - base : j - base + 1]
        root = lax.rsqrt(pivot)
        root = root * (1.5 - 0.5 * pivot * root * root)
        factor = jnp.where(row[base:] > j, column * (root * root), 0.0)
        lead = work[g0][j - base : j - base + 1]
        for g in range(g0, groups):
            work[g] = work[g] - factor[8 * (g - g0) : 8 * (g - g0) + 8] * lead
        for k in range(j + 1, BLK):
            skip = 8 * (k // 8 - g0)
            cols[k] = cols[k] - factor[skip:] * column[k - base : k - base + 1]
        scale[g0] = jnp.where(row8 == j - base, root, scale[g0])
    return jnp.concatenate([work[g] * scale[g] for g in range(groups)], axis=0)


def factor_panel(work):
    per_tile = 128 // BLK
    row = lax.broadcasted_iota(jnp.int32, (PW, BLK), 0)
    lane = lax.broadcasted_iota(jnp.int32, (BLK, 128), 1)

    def step(b, carry):
        low = pl.multiple_of(b * BLK, BLK)
        tile = pl.multiple_of((b // per_tile) * 128, 128)
        turn = (128 - (b % per_tile) * BLK) % 128
        columns = pltpu.roll(work[:, pl.ds(tile, 128)], turn, 1)
        block = pltpu.roll(work[pl.ds(low, BLK), pl.ds(tile, 128)], turn, 1)
        done = factor_diagonal(block)
        inverse = jnp.where(lane < BLK, pltpu.roll(done, 128 - BLK, 1), 0.0)
        upper = exact(inverse[:, :BLK], work[pl.ds(low, BLK), :])
        lead = exact(columns, inverse, NT)
        lead = jnp.where(row >= low + BLK, lead, 0.0)
        work[...] = work[...] - exact(lead, upper)
        work[pl.ds(low, BLK), :] = upper
        return carry

    lax.fori_loop(0, PW // BLK, step, 0)


def pivot_values(table, stride, share, along_rows):
    shape = (NPIV, 1) if along_rows else (1, NPIV)
    block = lax.broadcasted_iota(jnp.int32, shape, 0 if along_rows else 1) % PW // share
    values = jnp.zeros(shape, F32)
    for r in range(PW // share):
        values = jnp.where(block == r, table[r * stride], values)
    return values


def tile_values(table, start, count):
    return jnp.concatenate([jnp.full((1, TS), table[start + i], F32) for i in range(count)], axis=1)


def finish_panel(work, lower, inv_hi, inv_lo, inv_t_hi, inv_t_lo):
    row = lax.broadcasted_iota(jnp.int32, (PW, PW), 0)
    col = lax.broadcasted_iota(jnp.int32, (PW, PW), 1)
    lower[:PW, :] = jnp.where(col <= row, work[:, :PW].T, 0.0)
    inverse = work[:, PW:]
    inv_hi[...], inv_lo[...] = split(inverse)
    inv_t_hi[...], inv_t_lo[...] = split(inverse.T)
    return inverse


def unit():
    row = lax.broadcasted_iota(jnp.int32, (PW, PW), 0)
    col = lax.broadcasted_iota(jnp.int32, (PW, PW), 1)
    return jnp.where(row == col, 1.0, 0.0)


def first_kernel(sizes, place, group_of, kid_of, near, far,
                 lower, inv_hi, inv_lo, inv_t_hi, inv_t_lo, link_out, link_t, rest, piv_t, piv,
                 pile, wide, work):
    cols, fan, share, held, tiles = sizes
    my_row, my_col = place[0], place[1]
    my_q, my_a = my_row % fan, my_row // fan
    col_share = PW // cols
    for dq, source in enumerate((near, far)):
        for d in range(cols):
            r = (my_a ^ d) * fan + (my_q ^ dq)
            pieces = [source[c ^ my_col, d, :held, :] for c in range(cols)]
            line = jnp.concatenate(
                [piece[:, k * col_share : (k + 1) * col_share] for k in range(NP) for piece in pieces],
                axis=1,
            )
            kids = []
            for e in range(cols):
                packed = source[e, d, held:, :]
                kids += [packed[:, :held], packed[:, held:]]
            kids = jnp.concatenate(kids, axis=0).T
            for k in range(NP):
                at = pl.ds(pl.multiple_of(k * PW + r * share, share), share)
                pile[at, :] = line[k * share : (k + 1) * share]
                wide[at, :] = kids[k * share : (k + 1) * share]
    piv[...] = wide[...].astype(BF16)
    piv_t[...] = wide[...].T.astype(BF16)
    product = dot(piv[...], piv_t[...])
    same_group = pivot_values(group_of, tiles, share, True) == pivot_values(group_of, tiles, share, False)
    same_kid = pivot_values(kid_of, tiles, share, True) == pivot_values(kid_of, tiles, share, False)
    pile[...] = jnp.where(same_group, pile[...], 0.0) + jnp.where(same_kid, product, 0.0)
    work[:, :PW] = pile[:PW, :PW]
    work[:, PW:] = unit()
    factor_panel(work)
    inverse = finish_panel(work, lower, inv_hi, inv_lo, inv_t_hi, inv_t_lo)
    link = exact(pile[PW:, :PW], inverse, NT).astype(BF16)
    link_out[...] = link
    lower[PW:, :] = link.astype(F32)
    link_t[...] = link.astype(F32).T.astype(BF16)
    rest[...] = pile[PW:, PW:] - dot(link, link, NT)


def second_kernel(rest, lower, inv_hi, inv_lo, inv_t_hi, inv_t_lo, work):
    work[:, :PW] = rest[...]
    work[:, PW:] = unit()
    factor_panel(work)
    finish_panel(work, lower, inv_hi, inv_lo, inv_t_hi, inv_t_lo)


def place_kernel(sizes, place, inverse_map, held, *outs):
    cols, fan, tiles, slice_cols = sizes
    my_row, my_col = place[0], place[1]
    my_q = my_row % fan

    def fetch(block, i):
        tile = inverse_map[block * tiles + i]
        at = pl.multiple_of((tile % tiles) * TS, TS)
        return held[tile // tiles, :, pl.ds(at, TS)]

    for i in range(tiles):
        mine = fetch(my_row, i)
        for d in range(cols):
            outs[d][:slice_cols, i * TS : (i + 1) * TS] = mine
    for d in range(cols):
        for i in range(tiles):
            outs[d][slice_cols:, i * TS : (i + 1) * TS] = fetch((my_col ^ d) * fan + my_q, i)


def solve_rows(first, second, inv1_hi, inv1_lo, inv2_hi, inv2_lo, link):
    high, low = split(first)
    head = dot(high, inv1_hi) + dot(high, inv1_lo) + dot(low, inv1_hi)
    high, low = split(second - dot(head.astype(BF16), link))
    tail = dot(high, inv2_hi) + dot(high, inv2_lo) + dot(low, inv2_hi)
    return head, tail


def solve_cols(first, second, inv1_hi, inv1_lo, inv2_hi, inv2_lo, link):
    def apply(inv_hi, inv_lo, value):
        high, low = split(value)
        both = dot(jnp.concatenate([inv_hi, inv_lo], axis=0), high)
        return both[:PW] + both[PW:] + dot(inv_hi, low)

    head = apply(inv1_hi, inv1_lo, first)
    return head, apply(inv2_hi, inv2_lo, second - dot(link, head.astype(BF16)))


def schur_kernel(sizes, masks, place, group_of, kid_of, front, strips, near_kids, far_kids,
                 piv, piv_t, lower1, lower2, inv1_hi, inv1_lo, inv2_hi, inv2_lo, link,
                 inv1_t_hi, inv1_t_lo, inv2_t_hi, inv2_t_lo, link_t, *refs):
    rows, cols, fan, share, held, slice_cols, block_rows, local_rows, local_cols, tiles = sizes
    sources = refs[:cols]
    halves = [refs[cols : cols + 2], refs[cols + 2 : cols + 4]]
    out, panel, flipped, kids, strip, solved, pieces = refs[cols + 4 :]
    my_row, my_col = place[0], place[1]
    my_q = my_row % fan
    step = pl.program_id(0)
    first_tile = my_col * fan * tiles
    wide = strip.shape[1]

    @pl.when(step == 0)
    def _():
        for q in range(fan):

            @pl.when(my_q == q)
            def _():
                kids[:, q * local_rows : (q + 1) * local_rows] = near_kids[...]

            @pl.when(my_q != q)
            def _():
                kids[:, q * local_rows : (q + 1) * local_rows] = far_kids[...]

        group_col = pivot_values(group_of, tiles, share, True)
        kid_col = pivot_values(kid_of, tiles, share, True)

        def solve(n, carry):
            at = pl.ds(pl.multiple_of(n * wide, wide), wide)
            for r in range(rows):
                piece = strips[r, :, at].astype(F32)
                for k in range(NP):
                    low = k * PW + r * share
                    strip[low : low + share, :] = piece[k * share : (k + 1) * share]
            tile = first_tile + n * (wide // TS)
            group_all = tile_values(group_of, tile, wide // TS)
            kid_all = tile_values(kid_of, tile, wide // TS)
            product = dot(piv[...], kids[:, at])
            full = jnp.where(group_col == group_all, strip[...], 0.0) + jnp.where(
                kid_col == kid_all, product, 0.0
            )
            head, tail = solve_cols(
                full[:PW], full[PW:], inv1_hi[...], inv1_lo[...], inv2_hi[...], inv2_lo[...], link[...]
            )
            flipped[:PW, at] = (-head).astype(BF16)
            flipped[PW:, at] = (-tail).astype(BF16)
            return carry

        lax.fori_loop(0, local_cols // wide, solve, 0)

    for half in range(2):

        @pl.when(step // (pl.num_programs(0) // 2) == half)
        def _():
            for i, mask in enumerate(masks[half]):
                source = halves[half][i // (cols // 2)]
                pieces[my_col ^ mask] = source[i % (cols // 2)]

    col_share = PW // cols
    subs = block_rows // TS
    own_t = jnp.concatenate([source[:slice_cols, :] for source in sources], axis=0)
    own = own_t.astype(F32).T.astype(BF16)
    product = dot(own, piv_t[...])
    entries = jnp.concatenate(
        [pieces[c, :, k * col_share : (k + 1) * col_share] for k in range(NP) for c in range(cols)],
        axis=1,
    )
    group_row = pivot_values(group_of, tiles, share, False)
    kid_row = pivot_values(kid_of, tiles, share, False)
    my_tile = my_row * tiles + step * subs
    parts = []
    for i in range(subs):
        part = slice(i * TS, (i + 1) * TS)
        parts.append(
            jnp.where(group_row == group_of[my_tile + i], entries[part], 0.0)
            + jnp.where(kid_row == kid_of[my_tile + i], product[part], 0.0)
        )
    full = jnp.concatenate(parts, axis=0)
    head, tail = solve_rows(
        full[:, :PW], full[:, PW:], inv1_t_hi[...], inv1_t_lo[...], inv2_t_hi[...], inv2_t_lo[...], link_t[...]
    )
    solved[:, :PW] = head
    solved[:, PW:] = tail

    @pl.when(step == 0)
    def _():
        at = pl.multiple_of(my_row * share, share)
        solved[:share, :PW] = lower1[pl.ds(at, share), :]
        solved[:share, PW:] = jnp.zeros((share, PW), F32)
        solved[share : 2 * share, :PW] = lower1[pl.ds(PW + at, share), :]
        solved[share : 2 * share, PW:] = lower2[pl.ds(at, share), :]

    per_tile = 128 // col_share
    lane = lax.broadcasted_iota(jnp.int32, (block_rows, 128), 1)
    moved_out = jnp.zeros((block_rows, 128), F32)
    for k in range(NP):
        tile = pl.multiple_of(k * PW + (my_col // per_tile) * 128, 128)
        turn = (128 + k * col_share - (my_col % per_tile) * col_share) % 128
        moved = pltpu.roll(solved[:, pl.ds(tile, 128)], turn, 1)
        moved_out = jnp.where(lane // col_share == k, moved, moved_out)
    panel[...] = moved_out[:, : NP * col_share].astype(BF16)

    lead = solved[...].astype(BF16)
    span = min(512, local_cols)
    for n in range(local_cols // span):
        at = slice(n * span, (n + 1) * span)
        update = dot(lead, flipped[:, at])
        product = dot(own, kids[:, at])
        group_all = tile_values(group_of, first_tile + n * (span // TS), span // TS)
        kid_all = tile_values(kid_of, first_tile + n * (span // TS), span // TS)
        for i in range(subs):
            part = slice(i * TS, (i + 1) * TS)
            out[part, at] = (
                jnp.where(group_all == group_of[my_tile + i], front[part, at], 0.0)
                + jnp.where(kid_all == kid_of[my_tile + i], product[part], 0.0)
                + update[part]
            )
    for q in range(fan):
        out[:, q * local_rows : q * local_rows + held] = jnp.zeros((block_rows, held), F32)

    @pl.when(step == 0)
    def _():
        out[:held, :] = jnp.zeros((held, local_cols), F32)


def params():
    return pltpu.CompilerParams(vmem_limit_bytes=VMEM_BYTES)


def local(front_entries, tile_group, child_factor, row_map):
    rows, cols = lax.axis_size("row"), lax.axis_size("col")
    fan = rows // cols
    assert fan == 2
    local_rows, local_cols = front_entries.shape
    slice_cols = child_factor.shape[1]
    kid_cols = slice_cols * cols
    tiles = local_rows // TS
    share = PW // rows
    held = NP * share
    my_row, my_col = lax.axis_index("row"), lax.axis_index("col")
    place = jnp.stack([my_row, my_col]).astype(jnp.int32)

    flipped = child_factor.T
    own_map = lax.dynamic_slice_in_dim(row_map, my_row * tiles, tiles)
    starts = flipped.reshape(slice_cols, tiles, TS)[:, :, :held]

    def chosen(block):
        keep = (own_map == block * tiles)[None, :, None]
        return jnp.sum(jnp.where(keep, starts, 0), axis=1, dtype=F32)

    corner = jnp.concatenate(
        [
            front_entries[:held, q * local_rows + k * share : q * local_rows + (k + 1) * share]
            for k in range(NP)
            for q in range(fan)
        ],
        axis=1,
    )
    kids = jnp.concatenate([chosen(my_row), chosen(jnp.bitwise_xor(my_row, rows // 2))], axis=1)
    packet = jnp.concatenate([corner, kids], axis=0)
    packets = [swapped(packet, "row", d * fan) for d in range(cols)]

    row_strip = jnp.concatenate(
        [
            front_entries[:, q * local_rows + k * share : q * local_rows + (k + 1) * share]
            for k in range(NP)
            for q in range(fan)
        ],
        axis=1,
    )
    steps = [1 << i for i in range(cols.bit_length() - 1)]
    orders = [steps, steps[::-1]]
    halves = [row_strip[None, : local_rows // 2], row_strip[None, local_rows // 2 :]]
    masks = [[0], [0]]
    for h in range(2):
        for step in orders[h][:-1]:
            halves[h] = jnp.concatenate([halves[h], swapped(halves[h], "col", step)], axis=0)
            masks[h] = masks[h] + [m ^ step for m in masks[h]]
    gathered = lax.all_gather(flipped, "row", axis=0)
    col_strip, *packets = lax.optimization_barrier((front_entries[:held].astype(BF16), *packets))
    col_strips = lax.all_gather(col_strip, "row", axis=0)
    merged = []
    for d in range(cols):
        kid = packets[d][held:, :held] + packets[d ^ (cols // 2)][held:, held:]
        half = slice_cols // 2
        merged.append(
            jnp.concatenate(
                [packets[d][:held], jnp.concatenate([kid[:half], kid[half:]], axis=1)], axis=0
            )
        )
    merged = jnp.stack(merged)
    near = jnp.stack([swapped(merged, "col", d) for d in range(cols)])
    far = swapped(near, "row", 1)

    tile_ids = jnp.arange(row_map.shape[0], dtype=jnp.int32)
    inverse_map = jnp.sum(
        jnp.where(row_map[None, :] == tile_ids[:, None], tile_ids[None, :], 0), axis=1, dtype=jnp.int32
    )
    kid_of = (inverse_map >= row_map.shape[0] // 2).astype(F32)
    group_of = jnp.repeat(tile_group, MT // TS).astype(F32)

    placed = pl.pallas_call(
        functools.partial(place_kernel, (cols, fan, tiles, slice_cols)),
        out_shape=[jax.ShapeDtypeStruct((2 * slice_cols, local_rows), BF16)] * cols,
        in_specs=[smem_spec()] * 2 + [whole_spec()],
        out_specs=[whole_spec()] * cols,
        compiler_params=params(),
        cost_estimate=pl.CostEstimate(flops=0, bytes_accessed=8 * 2**20, transcendentals=0),
        name="place_tiles",
    )(place, inverse_map, gathered)
    near, far, *placed = lax.optimization_barrier((near, far, *placed))
    kid_parts = [swapped(placed[d], "col", d) for d in range(cols)]
    square = jax.ShapeDtypeStruct((PW, PW), BF16)
    lower1, inv1_hi, inv1_lo, inv1_t_hi, inv1_t_lo, link, link_t, rest, piv_t, piv = pl.pallas_call(
        functools.partial(first_kernel, (cols, fan, share, held, tiles)),
        out_shape=[
            jax.ShapeDtypeStruct((2 * PW, PW), F32),
            square, square, square, square, square, square,
            jax.ShapeDtypeStruct((PW, PW), F32),
            jax.ShapeDtypeStruct((kid_cols, NPIV), BF16),
            jax.ShapeDtypeStruct((NPIV, kid_cols), BF16),
        ],
        in_specs=[smem_spec()] * 3 + [whole_spec()] * 2,
        out_specs=[whole_spec()] * 10,
        scratch_shapes=[
            pltpu.VMEM((NPIV, NPIV), F32),
            pltpu.VMEM((NPIV, kid_cols), F32),
            pltpu.VMEM((PW, 2 * PW), F32),
        ],
        compiler_params=params(),
        cost_estimate=pl.CostEstimate(flops=2 * 10**10, bytes_accessed=5 * 10**7, transcendentals=0),
        name="first_pivots",
    )(place, group_of, kid_of, near, far)

    rest, *arrived = lax.optimization_barrier((rest, *kid_parts, *halves))
    kid_parts, halves = arrived[:cols], arrived[cols:]
    near_kids = jnp.concatenate([part[slice_cols:] for part in kid_parts], axis=0)
    rest, near_kids = lax.optimization_barrier((rest, near_kids))
    far_kids = swapped(near_kids, "row", 1)
    others = [swapped(halves[h], "col", orders[h][-1]) for h in range(2)]
    masks = [masks[h] + [m ^ orders[h][-1] for m in masks[h]] for h in range(2)]
    lower2, inv2_hi, inv2_lo, inv2_t_hi, inv2_t_lo = pl.pallas_call(
        second_kernel,
        out_shape=[jax.ShapeDtypeStruct((PW, PW), F32), square, square, square, square],
        in_specs=[whole_spec()],
        out_specs=[whole_spec()] * 5,
        scratch_shapes=[pltpu.VMEM((PW, 2 * PW), F32)],
        compiler_params=params(),
        cost_estimate=pl.CostEstimate(flops=2 * 10**10, bytes_accessed=5 * 10**7, transcendentals=0),
        name="second_pivots",
    )(rest)

    block_rows = min(256, local_rows // 2)
    per_half = local_rows // 2 // block_rows
    wide = min(1024, local_cols)
    piece = (cols // 2, block_rows, fan * held)
    schur_block, factor_panels = pl.pallas_call(
        functools.partial(
            schur_kernel,
            (rows, cols, fan, share, held, slice_cols, block_rows, local_rows, local_cols, tiles),
            masks,
        ),
        grid=(2 * per_half,),
        out_shape=[
            jax.ShapeDtypeStruct((local_rows, local_cols), F32),
            jax.ShapeDtypeStruct((local_rows, NP * PW // cols), BF16),
        ],
        in_specs=[smem_spec()] * 3
        + [pl.BlockSpec((block_rows, local_cols), lambda i: (i, 0))]
        + [whole_spec()] * 17
        + [pl.BlockSpec((2 * slice_cols, block_rows), lambda i: (0, i))] * cols
        + [pl.BlockSpec(piece, lambda i: (0, jnp.minimum(i, per_half - 1), 0))] * 2
        + [pl.BlockSpec(piece, lambda i: (0, jnp.maximum(i - per_half, 0), 0))] * 2,
        out_specs=[
            pl.BlockSpec((block_rows, local_cols), lambda i: (i, 0)),
            pl.BlockSpec((block_rows, NP * PW // cols), lambda i: (i, 0)),
        ],
        scratch_shapes=[
            pltpu.VMEM((NPIV, local_cols), BF16),
            pltpu.VMEM((kid_cols, local_cols), BF16),
            pltpu.VMEM((NPIV, wide), F32),
            pltpu.VMEM((block_rows, NPIV), F32),
            pltpu.VMEM((cols, block_rows, fan * held), F32),
        ],
        compiler_params=params(),
        cost_estimate=pl.CostEstimate(flops=3 * 10**10, bytes_accessed=9 * 10**7, transcendentals=0),
        name="schur_update",
    )(
        place, group_of, kid_of, front_entries, col_strips, near_kids, far_kids,
        piv, piv_t, lower1, lower2, inv1_hi, inv1_lo, inv2_hi, inv2_lo, link,
        inv1_t_hi, inv1_t_lo, inv2_t_hi, inv2_t_lo, link_t, *kid_parts,
        halves[0], others[0], halves[1], others[1],
    )
    return (factor_panels, schur_block)


def solution(mesh):
    placed = (P("row", "col"), P(), P("row", "col"), P())
    return jax.shard_map(
        local,
        mesh=mesh,
        in_specs=placed,
        out_specs=(P("row", "col"), P("row", "col")),
        check_vma=False,
    )
```

profile of v0, /device:TPU:0, one launch (start us, length us, event | category | flops | bytes accessed | tf_op | source)
XLA Modules:
  0.0 161.5 jit_solution(3811196634486328643)
XLA Ops:
  7.2 0.7 all-gather.7.cloned.1.call-update
  8.0 1.0 copy.6
  8.9 0.7 broadcast_compare_fusion
  10.1 0.9 fusion.2
  11.1 5.1 %collective-permute-start.2 = (f32[128,128]{1,0:T(8,128)S(1)}, f32[128,128]{1,0:T(8,128)S(1)}, u32[]{:S(2)}, u32[]{:S(2)}) collective-permute-start(f32[128,128]{1,0:T(8,128)S(1)} %maximum_maximum_fusion), channel_id=1, source_target_pairs={{0,24},{4,28},{8,16},{12,20},{16,8},{20,12},{24,0},{28,4},{1,25},{... | collective-permute-start | bytes 196616 | tf_op jit(solution)/shard_map/ppermute | solution.py:40
  16.2 0.6 collective-permute-start
  16.9 2.1 %slice.170 = bf16[64,4096]{1,0:T(8,128)(2,1)} slice(f32[2048,4096]{1,0:T(8,128)} %front.1), slice={[0:64], [0:4096]} | slice | bytes 1048576 | tf_op jit(solution)/shard_map/slice | solution.py:398
  19.0 2.9 %collective-permute-done.1 = f32[128,128]{1,0:T(8,128)S(1)} collective-permute-done((f32[128,128]{1,0:T(8,128)S(1)}, f32[128,128]{1,0:T(8,128)S(1)}, u32[]{:S(2)}, u32[]{:S(2)}) %collective-permute-start.1) | collective-permute-done | bytes 65568 | tf_op jit(solution)/shard_map/ppermute | solution.py:40
  21.9 2.9 %fusion.1 = (f32[2048,32]{1,0:T(8,128)S(1)}, f32[2048,32]{1,0:T(8,128)S(1)}, f32[2048,32]{1,0:T(8,128)S(1)}, f32[2048,32]{1,0:T(8,128)S(1)}) fusion(f32[2048,4096]{1,0:T(8,128)} %front.1), kind=kLoop, calls=%fused_computation.27 | loop fusion | bytes 2097152 | tf_op jit(solution)/shard_map/slice | solution.py:383
  24.8 0.9 pad_maximum_fusion
  26.2 1.6 collective-permute-start.4
  27.8 1.5 collective-permute-start.3
  29.8 1.6 collective-permute-start.11
  31.4 6.9 %collective-permute-done.4 = f32[4,96,128]{2,1,0:T(8,128)S(1)} collective-permute-done((f32[4,96,128]{2,1,0:T(8,128)S(1)}, f32[4,96,128]{2,1,0:T(8,128)S(1)}, u32[]{:S(2)}, u32[]{:S(2)}) %collective-permute-start.4) | collective-permute-done | bytes 196640 | tf_op jit(solution)/shard_map/ppermute | solution.py:40
  38.3 0.9 pad_maximum_fusion.4.near
  39.2 1.6 %collective-permute-start.10 = (f32[1,1024,128]{2,1,0:T(8,128)S(1)}, f32[1,1024,128]{2,1,0:T(8,128)}, u32[]{:S(2)}, u32[]{:S(2)}) collective-permute-start(f32[1,1024,128]{2,1,0:T(8,128)S(1)} %get-tuple-element.95), channel_id=1, source_target_pairs={{0,1},{1,0},{2,3},{3,2},{4,5},{5,4},{6,7},{7,6},{8,9},{9,8},{10,11... | collective-permute-start | bytes 1572872 | tf_op jit(solution)/shard_map/ppermute | solution.py:40
  41.5 0.7 convert_element_type.19.group_of
  42.9 5.2 %collective-permute-done.11 = f32[1,1024,128]{2,1,0:T(8,128)S(1)} collective-permute-done((f32[1,1024,128]{2,1,0:T(8,128)S(1)}, f32[1,1024,128]{2,1,0:T(8,128)S(1)}, u32[]{:S(2)}, u32[]{:S(2)}) %collective-permute-start.11) | collective-permute-done | bytes 524320 | tf_op jit(solution)/shard_map/ppermute | solution.py:40
  48.2 5.4 %collective-permute-done.10 = f32[1,1024,128]{2,1,0:T(8,128)} collective-permute-done((f32[1,1024,128]{2,1,0:T(8,128)S(1)}, f32[1,1024,128]{2,1,0:T(8,128)}, u32[]{:S(2)}, u32[]{:S(2)}) %collective-permute-start.10) | collective-permute-done | bytes 524320 | tf_op jit(solution)/shard_map/ppermute | solution.py:40
  53.6 1.1 pad_maximum_fusion.1.refs_4_
  54.8 4.0 %place_tiles.1 = (bf16[128,2048]{1,0:T(8,128)(2,1)}, bf16[128,2048]{1,0:T(8,128)(2,1)}, bf16[128,2048]{1,0:T(8,128)(2,1)}, bf16[128,2048]{1,0:T(8,128)(2,1)}) custom-call(s32[2]{0:T(128)} %pad_add_fusion.place, s32[128]{0:T(128)} %copy-done.7, bf16[8,64,2048]{2,1,0:T(8,128)(2,1)} %bitcast.24), custom_call_target="tpu_custom_call" | custom-call | bytes 8388608 | tf_op jit(solution)/shard_map/place_tiles/pallas_call | solution.py:420
  58.8 1.7 %collective-permute-start.7 = (bf16[128,2048]{1,0:T(8,128)(2,1)}, bf16[128,2048]{1,0:T(8,128)(2,1)S(1)}, u32[]{:S(2)}, u32[]{:S(2)}) collective-permute-start(bf16[128,2048]{1,0:T(8,128)(2,1)} %get-tuple-element.56), channel_id=1, source_target_pairs={{0,1},{1,0},{2,3},{3,2},{4,5},{5,4},{6,7},{7,6},{8,9},{9,8},{10,11... | collective-permute-start | bytes 1572872 | tf_op jit(solution)/shard_map/ppermute | solution.py:40
  60.5 1.5 collective-permute-start.8
  62.4 19.4 %first_pivots.1 = (f32[512,256]{1,0:T(8,128)}, bf16[256,256]{1,0:T(8,128)(2,1)}, bf16[256,256]{1,0:T(8,128)(2,1)}, bf16[256,256]{1,0:T(8,128)(2,1)}, bf16[256,25...) custom-call(s32[2]{0:T(128)} %pad_add_fusion.place, ...), custom_call_target="tpu_custom_call" | custom-call | flops 20000000000 | bytes 50000000 | tf_op jit(solution)/shard_map/first_pivots/pallas_call | solution.py:432
  81.8 3.5 %collective-permute-done.8.refs_2_ = bf16[128,2048]{1,0:T(8,128)(2,1)S(1)} collective-permute-done((bf16[128,2048]{1,0:T(8,128)(2,1)}, bf16[128,2048]{1,0:T(8,128)(2,1)S(1)}, u32[]{:S(2)}, u32[]{:S(2)}) %collective-permute-start.8) | collective-permute-done | bytes 524320 | tf_op jit(solution)/shard_map/ppermute | solution.py:40
  85.3 0.7 copy-done.5
  86.0 1.0 slice.144
  87.2 1.6 collective-permute-start.13
  89.4 16.8 %second_pivots.1 = (f32[256,256]{1,0:T(8,128)}, bf16[256,256]{1,0:T(8,128)(2,1)}, bf16[256,256]{1,0:T(8,128)(2,1)}, bf16[256,256]{1,0:T(8,128)(2,1)}, bf16[256,256]{1,0:T(8,128)(2,1)}) custom-call(f32[256,256]{1,0:T(8,128)} %get-tuple-element.68.rest), custom_call_target="tpu_custom_call" | custom-call | flops 20000000000 | bytes 50000000 | tf_op jit(solution)/shard_map/second_pivots/pallas_call | solution.py:460
  106.2 6.7 %collective-permute-done.13.refs_5_ = f32[2,1024,128]{2,1,0:T(8,128)} collective-permute-done((f32[2,1024,128]{2,1,0:T(8,128)S(1)}, f32[2,1024,128]{2,1,0:T(8,128)}, u32[]{:S(2)}, u32[]{:S(2)}) %collective-permute-start.13) | collective-permute-done | bytes 1048608 | tf_op jit(solution)/shard_map/ppermute | solution.py:40
  112.9 1.3 collective-permute-done.14.refs_7_
  114.2 40.4 %schur_update.1 = (f32[2048,4096]{1,0:T(8,128)}, bf16[2048,128]{1,0:T(8,128)(2,1)}) custom-call(s32[2]{0:T(128)} %pad_add_fusion.place, f32[128]{0:T(128)} %convert_element_type.19.group_of, f32[128]{0:T(128)} %compare_convert_fusion.kid_of, f32[2048,4096]{1,0:T(8,128)} %front.1, bf16[8,64,4096]{2,1,0:T(8,128)(2,1)} %bitcast.31, ...), custom_call_target="tpu_custom_call" | custom-call | flops 30000001024 | bytes 90000000 | tf_op jit(solution)/shard_map/schur_update/pallas_call | solution.py:475
  (63 shorter events, 4.2 us)
Async XLA Ops:
  7.2 47.6 %all-gather.7.cloned.1.call-start = ((), (), s32[]{:S(2)}) async-start(), calls=%async_computation.1 | async-start | bytes 2359296 | tf_op jit(solution)/shard_map/all_gather | solution.py:397
  7.9 106.3 %all-gather.5.cloned.1.call-start = ((), (), s32[]{:S(2)}) async-start(), calls=%async_computation | async-start | bytes 4718592 | tf_op jit(solution)/shard_map/all_gather | solution.py:399
  11.1 7.8 %collective-permute-start.2 = (f32[128,128]{1,0:T(8,128)S(1)}, f32[128,128]{1,0:T(8,128)S(1)}, u32[]{:S(2)}, u32[]{:S(2)}) collective-permute-start(f32[128,128]{1,0:T(8,128)S(1)} %maximum_maximum_fusion), channel_id=1, source_target_pairs={{0,24},{4,28},{8,16},{12,20},{16,8},{20,12},{24,0},{28,4},{1,25},{... | collective-permute-start | bytes 196616 | tf_op jit(solution)/shard_map/ppermute | solution.py:40
  16.2 5.6 %collective-permute-start.1 = (f32[128,128]{1,0:T(8,128)S(1)}, f32[128,128]{1,0:T(8,128)S(1)}, u32[]{:S(2)}, u32[]{:S(2)}) collective-permute-start(f32[128,128]{1,0:T(8,128)S(1)} %maximum_maximum_fusion), channel_id=1, source_target_pairs={{0,16},{4,20},{8,24},{12,28},{16,0},{20,4},{24,8},{28,12},{1,17},{... | collective-permute-start | bytes 196616 | tf_op jit(solution)/shard_map/ppermute | solution.py:40
  16.2 5.6 %collective-permute-start = (f32[128,128]{1,0:T(8,128)S(1)}, f32[128,128]{1,0:T(8,128)S(1)}, u32[]{:S(2)}, u32[]{:S(2)}) collective-permute-start(f32[128,128]{1,0:T(8,128)S(1)} %maximum_maximum_fusion), channel_id=1, source_target_pairs={{0,8},{4,12},{8,0},{12,4},{16,24},{20,28},{24,16},{28,20},{1,9},{5... | collective-permute-start | bytes 196616 | tf_op jit(solution)/shard_map/ppermute | solution.py:40
  26.1 15.3 %copy-start.8 = (s32[32]{0:T(128)S(1)}, s32[32]{0:T(128)}, u32[]{:S(2)}) copy-start(s32[32]{0:T(128)} %param.5) | copy-start | bytes 388
  26.1 16.1 %copy-start.6 = (s32[128]{0:T(128)S(1)}, s32[128]{0:T(128)}, u32[]{:S(2)}) copy-start(s32[128]{0:T(128)} %param.7) | copy-start | bytes 1540
  26.2 12.1 %collective-permute-start.4 = (f32[4,96,128]{2,1,0:T(8,128)S(1)}, f32[4,96,128]{2,1,0:T(8,128)S(1)}, u32[]{:S(2)}, u32[]{:S(2)}) collective-permute-start(f32[4,96,128]{2,1,0:T(8,128)S(1)} %get-tuple-element.97), channel_id=1, source_target_pairs={{0,2},{1,3},{2,0},{3,1},{4,6},{5,7},{6,4},{7,5},{8,10},{9,11},{10,... | collective-permute-start | bytes 589832 | tf_op jit(solution)/shard_map/ppermute | solution.py:40
  27.8 10.5 %collective-permute-start.3 = (f32[4,96,128]{2,1,0:T(8,128)S(1)}, f32[4,96,128]{2,1,0:T(8,128)S(1)}, u32[]{:S(2)}, u32[]{:S(2)}) collective-permute-start(f32[4,96,128]{2,1,0:T(8,128)S(1)} %get-tuple-element.97), channel_id=1, source_target_pairs={{0,1},{1,0},{2,3},{3,2},{4,5},{5,4},{6,7},{7,6},{8,9},{9,8},{10,11... | collective-permute-start | bytes 589832 | tf_op jit(solution)/shard_map/ppermute | solution.py:40
  29.3 9.0 %collective-permute-start.5 = (f32[4,96,128]{2,1,0:T(8,128)S(1)}, f32[4,96,128]{2,1,0:T(8,128)S(1)}, u32[]{:S(2)}, u32[]{:S(2)}) collective-permute-start(f32[4,96,128]{2,1,0:T(8,128)S(1)} %get-tuple-element.97), channel_id=1, source_target_pairs={{0,3},{1,2},{2,1},{3,0},{4,7},{5,6},{6,5},{7,4},{8,11},{9,10},{10,... | collective-permute-start | bytes 589832 | tf_op jit(solution)/shard_map/ppermute | solution.py:40
  29.8 18.4 %collective-permute-start.11 = (f32[1,1024,128]{2,1,0:T(8,128)S(1)}, f32[1,1024,128]{2,1,0:T(8,128)S(1)}, u32[]{:S(2)}, u32[]{:S(2)}) collective-permute-start(f32[1,1024,128]{2,1,0:T(8,128)S(1)} %get-tuple-element.94), channel_id=1, source_target_pairs={{0,2},{1,3},{2,0},{3,1},{4,6},{5,7},{6,4},{7,5},{8,10},{9,11},{10,... | collective-permute-start | bytes 1572872 | tf_op jit(solution)/shard_map/ppermute | solution.py:40
  39.2 19.6 %collective-permute-start.6 = (f32[4,4,96,128]{3,2,1,0:T(8,128)}, f32[4,4,96,128]{3,2,1,0:T(8,128)}, u32[]{:S(2)}, u32[]{:S(2)}) collective-permute-start(f32[4,4,96,128]{3,2,1,0:T(8,128)} %pad_maximum_fusion.4.near), channel_id=1, source_target_pairs={{0,4},{4,0},{8,12},{12,8},{16,20},{20,16},{24,28},{28,24},{1,5},{5... | collective-permute-start | bytes 2359304 | tf_op jit(solution)/shard_map/ppermute | solution.py:40
  39.2 14.4 %collective-permute-start.10 = (f32[1,1024,128]{2,1,0:T(8,128)S(1)}, f32[1,1024,128]{2,1,0:T(8,128)}, u32[]{:S(2)}, u32[]{:S(2)}) collective-permute-start(f32[1,1024,128]{2,1,0:T(8,128)S(1)} %get-tuple-element.95), channel_id=1, source_target_pairs={{0,1},{1,0},{2,3},{3,2},{4,5},{5,4},{6,7},{7,6},{8,9},{9,8},{10,11... | collective-permute-start | bytes 1572872 | tf_op jit(solution)/shard_map/ppermute | solution.py:40
  42.3 12.4 %copy-start.7 = (s32[128]{0:T(128)}, s32[128]{0:T(128)S(1)}, u32[]{:S(2)}) copy-start(s32[128]{0:T(128)S(1)} %select_reduce_fusion.inverse_map) | copy-start | bytes 1540
  48.2 40.6 %copy-start = (f32[2,1024,128]{2,1,0:T(8,128)}, f32[2,1024,128]{2,1,0:T(8,128)S(1)}, u32[]{:S(2)}) copy-start(f32[2,1024,128]{2,1,0:T(8,128)S(1)} %pad_maximum_fusion.2.refs_6_) | copy-start | bytes 3145732
  54.8 32.5 %copy-start.1 = (f32[2,1024,128]{2,1,0:T(8,128)}, f32[2,1024,128]{2,1,0:T(8,128)S(1)}, u32[]{:S(2)}) copy-start(f32[2,1024,128]{2,1,0:T(8,128)S(1)} %pad_maximum_fusion.1.refs_4_) | copy-start | bytes 3145732
  58.8 26.4 %copy-start.3 = (bf16[128,2048]{1,0:T(8,128)(2,1)S(1)}, bf16[128,2048]{1,0:T(8,128)(2,1)}, u32[]{:S(2)}) copy-start(bf16[128,2048]{1,0:T(8,128)(2,1)} %get-tuple-element.60.refs_0_) | copy-start | bytes 1572868
  58.8 22.9 %collective-permute-start.7 = (bf16[128,2048]{1,0:T(8,128)(2,1)}, bf16[128,2048]{1,0:T(8,128)(2,1)S(1)}, u32[]{:S(2)}, u32[]{:S(2)}) collective-permute-start(bf16[128,2048]{1,0:T(8,128)(2,1)} %get-tuple-element.56), channel_id=1, source_target_pairs={{0,1},{1,0},{2,3},{3,2},{4,5},{5,4},{6,7},{7,6},{8,9},{9,8},{10,11... | collective-permute-start | bytes 1572872 | tf_op jit(solution)/shard_map/ppermute | solution.py:40
  60.5 24.7 %collective-permute-start.8 = (bf16[128,2048]{1,0:T(8,128)(2,1)}, bf16[128,2048]{1,0:T(8,128)(2,1)S(1)}, u32[]{:S(2)}, u32[]{:S(2)}) collective-permute-start(bf16[128,2048]{1,0:T(8,128)(2,1)} %get-tuple-element.57), channel_id=1, source_target_pairs={{0,2},{1,3},{2,0},{3,1},{4,6},{5,7},{6,4},{7,5},{8,10},{9,11},{10,... | collective-permute-start | bytes 1572872 | tf_op jit(solution)/shard_map/ppermute | solution.py:40
  62.0 23.2 %collective-permute-start.9 = (bf16[128,2048]{1,0:T(8,128)(2,1)}, bf16[128,2048]{1,0:T(8,128)(2,1)}, u32[]{:S(2)}, u32[]{:S(2)}) collective-permute-start(bf16[128,2048]{1,0:T(8,128)(2,1)} %get-tuple-element.58), channel_id=1, source_target_pairs={{0,3},{1,2},{2,1},{3,0},{4,7},{5,6},{6,5},{7,4},{8,11},{9,10},{10,... | collective-permute-start | bytes 1572872 | tf_op jit(solution)/shard_map/ppermute | solution.py:40
  81.7 3.6 %copy-start.4 = (bf16[128,2048]{1,0:T(8,128)(2,1)}, bf16[128,2048]{1,0:T(8,128)(2,1)S(1)}, u32[]{:S(2)}) copy-start(bf16[128,2048]{1,0:T(8,128)(2,1)S(1)} %collective-permute-done.7.refs_1_) | copy-start | bytes 1572868
  85.2 0.8 copy-start.5
  87.1 19.0 %copy-start.2 = (bf16[256,2048]{1,0:T(8,128)(2,1)}, bf16[256,2048]{1,0:T(8,128)(2,1)S(1)}, u32[]{:S(2)}) copy-start(bf16[256,2048]{1,0:T(8,128)(2,1)S(1)} %pad_maximum_fusion.3.near_kids) | copy-start | bytes 3145732
  87.1 19.0 %collective-permute-start.12 = (bf16[256,2048]{1,0:T(8,128)(2,1)S(1)}, bf16[256,2048]{1,0:T(8,128)(2,1)}, u32[]{:S(2)}, u32[]{:S(2)}) collective-permute-start(bf16[256,2048]{1,0:T(8,128)(2,1)S(1)} %pad_maximum_fusion.3.near_kids), channel_id=1, source_target_pairs={{0,4},{4,0},{8,12},{12,8},{16,20},{20,16},{24,28},{28,24},{1,5},{5... | collective-permute-start | bytes 3145736 | tf_op jit(solution)/shard_map/ppermute | solution.py:40
  87.2 25.7 %collective-permute-start.13 = (f32[2,1024,128]{2,1,0:T(8,128)S(1)}, f32[2,1024,128]{2,1,0:T(8,128)}, u32[]{:S(2)}, u32[]{:S(2)}) collective-permute-start(f32[2,1024,128]{2,1,0:T(8,128)S(1)} %pad_maximum_fusion.1.refs_4_), channel_id=1, source_target_pairs={{0,2},{1,3},{2,0},{3,1},{4,6},{5,7},{6,4},{7,5},{8,10},{9,11},{10,... | collective-permute-start | bytes 3145736 | tf_op jit(solution)/shard_map/ppermute | solution.py:40
  88.8 25.3 %collective-permute-start.14 = (f32[2,1024,128]{2,1,0:T(8,128)S(1)}, f32[2,1024,128]{2,1,0:T(8,128)}, u32[]{:S(2)}, u32[]{:S(2)}) collective-permute-start(f32[2,1024,128]{2,1,0:T(8,128)S(1)} %pad_maximum_fusion.2.refs_6_), channel_id=1, source_target_pairs={{0,1},{1,0},{2,3},{3,2},{4,5},{5,4},{6,7},{7,6},{8,9},{9,8},{10,11... | collective-permute-start | bytes 3145736 | tf_op jit(solution)/shard_map/ppermute | solution.py:40
Sparse Core Ops, SparseCore 0:
  9.6 32.0 all-gather.6
  43.9 46.9 all-gather.4
where the time goes:
time: 162 us; the launch traced here: 161 us
  Pallas kernels  80.6 us (50%)
  waiting for transfers between devices  32.6 us (20%)
  starting transfers between devices  18.3 us (11%)
  between operations  14.3 us (9%)
  local copies, waits for them, and re-layouts  9.54 us (6%)
  other arithmetic  6.05 us (4%)
    pallas_call x1, Pallas kernels, local(): pl.pallas_call(functools.partial(schur_kernel, (rows, cols, fan, share, h...  40.4 us
    ppermute x15, waiting for transfers between devices, swapped(): lax.ppermute(value, axis, [(i, i ^ mask) for i in range(lax.axis_size(axi...  31.9 us
    pallas_call x1, Pallas kernels, local(): pl.pallas_call(functools.partial(first_kernel, (cols, fan, share, held, t...  19.4 us
    ppermute x15, starting transfers between devices, swapped(): lax.ppermute(value, axis, [(i, i ^ mask) for i in range(lax.axis_size(axi...  18.3 us
    pallas_call x1, Pallas kernels, local(): pl.pallas_call(second_kernel, out_shape=[jax.ShapeDtypeStruct((PW, PW), F...  16.8 us
    pallas_call x1, Pallas kernels, local(): pl.pallas_call(functools.partial(place_kernel, (cols, fan, tiles, slice_c...  3.99 us
  transfers between devices with their start and end apart: 17, of which 7 were waited for; matrix products, arithmetic and copies ran while one was open for 9% of the time, Pallas kernels for 25%

commit v1 on v0

--- a/solution.py
+++ b/solution.py
@@ -42,6 +42,10 @@
 
 def whole_spec():
     return pl.BlockSpec(memory_space=pltpu.VMEM)
+
+
+def any_spec():
+    return pl.BlockSpec(memory_space=pl.ANY)
 
 
 def smem_spec():
@@ -207,138 +211,203 @@
 
 def solve_cols(first, second, inv1_hi, inv1_lo, inv2_hi, inv2_lo, link):
     def apply(inv_hi, inv_lo, value):
-        high, low = split(value)
-        both = dot(jnp.concatenate([inv_hi, inv_lo], axis=0), high)
-        return both[:PW] + both[PW:] + dot(inv_hi, low)
+        both = dot(jnp.concatenate([inv_hi, inv_lo], axis=0), value.astype(BF16))
+        return both[:PW] + both[PW:]
 
     head = apply(inv1_hi, inv1_lo, first)
     return head, apply(inv2_hi, inv2_lo, second - dot(link, head.astype(BF16)))
 
 
-def schur_kernel(sizes, masks, place, group_of, kid_of, front, strips, near_kids, far_kids,
+def schur_kernel(sizes, masks, place, group_of, kid_of,
                  piv, piv_t, lower1, lower2, inv1_hi, inv1_lo, inv2_hi, inv2_lo, link,
                  inv1_t_hi, inv1_t_lo, inv2_t_hi, inv2_t_lo, link_t, *refs):
-    rows, cols, fan, share, held, slice_cols, block_rows, local_rows, local_cols, tiles = sizes
-    sources = refs[:cols]
-    halves = [refs[cols : cols + 2], refs[cols + 2 : cols + 4]]
-    out, panel, flipped, kids, strip, solved, pieces = refs[cols + 4 :]
+    rows, cols, fan, share, held, slice_cols, block_rows, local_rows, local_cols, tiles, wide = sizes
+    front, strips, near_kids, far_kids = refs[:4]
+    sources = refs[4 : 4 + cols]
+    halves = [refs[4 + cols : 6 + cols], refs[6 + cols : 8 + cols]]
+    out, panel = refs[8 + cols : 10 + cols]
+    (fronts, outs, strips_in, kids, own_t, pieces, flipped, strip, solved,
+     front_sems, out_sems, strip_sems, kid_sems, own_sems, piece_sems) = refs[10 + cols :]
     my_row, my_col = place[0], place[1]
     my_q = my_row % fan
-    step = pl.program_id(0)
     first_tile = my_col * fan * tiles
-    wide = strip.shape[1]
-
-    @pl.when(step == 0)
-    def _():
-        for q in range(fan):
-
-            @pl.when(my_q == q)
-            def _():
-                kids[:, q * local_rows : (q + 1) * local_rows] = near_kids[...]
-
-            @pl.when(my_q != q)
-            def _():
-                kids[:, q * local_rows : (q + 1) * local_rows] = far_kids[...]
-
-        group_col = pivot_values(group_of, tiles, share, True)
-        kid_col = pivot_values(kid_of, tiles, share, True)
-
-        def solve(n, carry):
-            at = pl.ds(pl.multiple_of(n * wide, wide), wide)
-            for r in range(rows):
-                piece = strips[r, :, at].astype(F32)
-                for k in range(NP):
-                    low = k * PW + r * share
-                    strip[low : low + share, :] = piece[k * share : (k + 1) * share]
-            tile = first_tile + n * (wide // TS)
-            group_all = tile_values(group_of, tile, wide // TS)
-            kid_all = tile_values(kid_of, tile, wide // TS)
-            product = dot(piv[...], kids[:, at])
-            full = jnp.where(group_col == group_all, strip[...], 0.0) + jnp.where(
-                kid_col == kid_all, product, 0.0
-            )
-            head, tail = solve_cols(
-                full[:PW], full[PW:], inv1_hi[...], inv1_lo[...], inv2_hi[...], inv2_lo[...], link[...]
-            )
-            flipped[:PW, at] = (-head).astype(BF16)
-            flipped[PW:, at] = (-tail).astype(BF16)
-            return carry
-
-        lax.fori_loop(0, local_cols // wide, solve, 0)
-
-    for half in range(2):
-
-        @pl.when(step // (pl.num_programs(0) // 2) == half)
+    steps = local_rows // block_rows
+    chunks = local_cols // wide
+    ins, holds = fronts.shape[0], outs.shape[0]
+    half_rows = local_rows // 2
+
+    def rows_at(i):
+        return pl.ds(pl.multiple_of(i * block_rows, block_rows), block_rows)
+
+    def front_copy(i, slot):
+        return pltpu.make_async_copy(front.at[rows_at(i), :], fronts.at[slot], front_sems.at[slot])
+
+    def out_copy(i, slot):
+        return pltpu.make_async_copy(outs.at[slot], out.at[rows_at(i), :], out_sems.at[slot])
+
+    def chunk_at(n):
+        return pl.ds(pl.multiple_of(n * wide, wide), wide)
+
+    def strip_copy(n):
+        return pltpu.make_async_copy(
+            strips.at[:, :, chunk_at(n)], strips_in.at[:, :, chunk_at(n)], strip_sems.at[n]
+        )
+
+    kid_copies = [
+        pltpu.make_async_copy(
+            source,
+            kids.at[:, pl.ds(pl.multiple_of((my_q ^ q) * local_rows, local_rows), local_rows)],
+            kid_sems.at[q],
+        )
+        for q, source in enumerate((near_kids, far_kids))
+    ]
+    own_copies = [
+        pltpu.make_async_copy(
+            source.at[:slice_cols, :], own_t.at[d * slice_cols : (d + 1) * slice_cols, :], own_sems.at[d]
+        )
+        for d, source in enumerate(sources)
+    ]
+    piece_copies = [
+        pltpu.make_async_copy(
+            halves[half][i // (cols // 2)].at[i % (cols // 2)],
+            pieces.at[my_col ^ mask, half * half_rows : (half + 1) * half_rows, :],
+            piece_sems.at[half * cols + i],
+        )
+        for half in range(2)
+        for i, mask in enumerate(masks[half])
+    ]
+    for copy in kid_copies:
+        copy.start()
+    for n in range(chunks):
+        strip_copy(n).start()
+    for copy in own_copies + piece_copies:
+        copy.start()
+    for copy in kid_copies:
+        copy.wait()
+    group_col = pivot_values(group_of, tiles, share, True)
+    kid_col = pivot_values(kid_of, tiles, share, True)
+
+    def solve(n, carry):
+        strip_copy(n).wait()
+
+        @pl.when(n == 0)
         def _():
-            for i, mask in enumerate(masks[half]):
-                source = halves[half][i // (cols // 2)]
-                pieces[my_col ^ mask] = source[i % (cols // 2)]
-
+            for i in range(ins):
+                front_copy(i, i).start()
+
+        at = chunk_at(n)
+        for r in range(rows):
+            piece = strips_in[r, :, at].astype(F32)
+            for k in range(NP):
+                low = k * PW + r * share
+                strip[low : low + share, :] = piece[k * share : (k + 1) * share]
+        tile = first_tile + n * (wide // TS)
+        group_all = tile_values(group_of, tile, wide // TS)
+        kid_all = tile_values(kid_of, tile, wide // TS)
+        product = dot(piv[...], kids[:, at])
+        full = jnp.where(group_col == group_all, strip[...], 0.0) + jnp.where(
+            kid_col == kid_all, product, 0.0
+        )
+        head, tail = solve_cols(
+            full[:PW], full[PW:], inv1_hi[...], inv1_lo[...], inv2_hi[...], inv2_lo[...], link[...]
+        )
+        flipped[:PW, at] = (-head).astype(BF16)
+        flipped[PW:, at] = (-tail).astype(BF16)
+        return carry
+
+    lax.fori_loop(0, chunks, solve, 0)
+    for copy in own_copies + piece_copies:
+        copy.wait()
     col_share = PW // cols
     subs = block_rows // TS
-    own_t = jnp.concatenate([source[:slice_cols, :] for source in sources], axis=0)
-    own = own_t.astype(F32).T.astype(BF16)
-    product = dot(own, piv_t[...])
-    entries = jnp.concatenate(
-        [pieces[c, :, k * col_share : (k + 1) * col_share] for k in range(NP) for c in range(cols)],
-        axis=1,
-    )
+    per_tile = 128 // col_share
+    span = min(512, local_cols)
     group_row = pivot_values(group_of, tiles, share, False)
     kid_row = pivot_values(kid_of, tiles, share, False)
-    my_tile = my_row * tiles + step * subs
-    parts = []
-    for i in range(subs):
-        part = slice(i * TS, (i + 1) * TS)
-        parts.append(
-            jnp.where(group_row == group_of[my_tile + i], entries[part], 0.0)
-            + jnp.where(kid_row == kid_of[my_tile + i], product[part], 0.0)
-        )
-    full = jnp.concatenate(parts, axis=0)
-    head, tail = solve_rows(
-        full[:, :PW], full[:, PW:], inv1_t_hi[...], inv1_t_lo[...], inv2_t_hi[...], inv2_t_lo[...], link_t[...]
-    )
-    solved[:, :PW] = head
-    solved[:, PW:] = tail
-
-    @pl.when(step == 0)
-    def _():
-        at = pl.multiple_of(my_row * share, share)
-        solved[:share, :PW] = lower1[pl.ds(at, share), :]
-        solved[:share, PW:] = jnp.zeros((share, PW), F32)
-        solved[share : 2 * share, :PW] = lower1[pl.ds(PW + at, share), :]
-        solved[share : 2 * share, PW:] = lower2[pl.ds(at, share), :]
-
-    per_tile = 128 // col_share
     lane = lax.broadcasted_iota(jnp.int32, (block_rows, 128), 1)
-    moved_out = jnp.zeros((block_rows, 128), F32)
-    for k in range(NP):
-        tile = pl.multiple_of(k * PW + (my_col // per_tile) * 128, 128)
-        turn = (128 + k * col_share - (my_col % per_tile) * col_share) % 128
-        moved = pltpu.roll(solved[:, pl.ds(tile, 128)], turn, 1)
-        moved_out = jnp.where(lane // col_share == k, moved, moved_out)
-    panel[...] = moved_out[:, : NP * col_share].astype(BF16)
-
-    lead = solved[...].astype(BF16)
-    span = min(512, local_cols)
-    for n in range(local_cols // span):
-        at = slice(n * span, (n + 1) * span)
-        update = dot(lead, flipped[:, at])
-        product = dot(own, kids[:, at])
-        group_all = tile_values(group_of, first_tile + n * (span // TS), span // TS)
-        kid_all = tile_values(kid_of, first_tile + n * (span // TS), span // TS)
+
+    def work_rows(step, carry):
+        own = own_t[:, rows_at(step)].astype(F32).T.astype(BF16)
+        product = dot(own, piv_t[...])
+        entries = jnp.concatenate(
+            [
+                pieces[c, rows_at(step), k * col_share : (k + 1) * col_share]
+                for k in range(NP)
+                for c in range(cols)
+            ],
+            axis=1,
+        )
+        my_tile = my_row * tiles + step * subs
+        parts = []
         for i in range(subs):
             part = slice(i * TS, (i + 1) * TS)
-            out[part, at] = (
-                jnp.where(group_all == group_of[my_tile + i], front[part, at], 0.0)
-                + jnp.where(kid_all == kid_of[my_tile + i], product[part], 0.0)
-                + update[part]
+            parts.append(
+                jnp.where(group_row == group_of[my_tile + i], entries[part], 0.0)
+                + jnp.where(kid_row == kid_of[my_tile + i], product[part], 0.0)
             )
-    for q in range(fan):
-        out[:, q * local_rows : q * local_rows + held] = jnp.zeros((block_rows, held), F32)
-
-    @pl.when(step == 0)
-    def _():
-        out[:held, :] = jnp.zeros((held, local_cols), F32)
+        full = jnp.concatenate(parts, axis=0)
+        head, tail = solve_rows(
+            full[:, :PW], full[:, PW:],
+            inv1_t_hi[...], inv1_t_lo[...], inv2_t_hi[...], inv2_t_lo[...], link_t[...],
+        )
+        solved[:, :PW] = head
+        solved[:, PW:] = tail
+
+        @pl.when(step == 0)
+        def _():
+            at = pl.multiple_of(my_row * share, share)
+            solved[:share, :PW] = lower1[pl.ds(at, share), :]
+            solved[:share, PW:] = jnp.zeros((share, PW), F32)
+            solved[share : 2 * share, :PW] = lower1[pl.ds(PW + at, share), :]
+            solved[share : 2 * share, PW:] = lower2[pl.ds(at, share), :]
+
+        moved_out = jnp.zeros((block_rows, 128), F32)
+        for k in range(NP):
+            tile = pl.multiple_of(k * PW + (my_col // per_tile) * 128, 128)
+            turn = (128 + k * col_share - (my_col % per_tile) * col_share) % 128
+            moved = pltpu.roll(solved[:, pl.ds(tile, 128)], turn, 1)
+            moved_out = jnp.where(lane // col_share == k, moved, moved_out)
+        panel[rows_at(step), :] = moved_out[:, : NP * col_share].astype(BF16)
+
+        slot, hold = step % ins, step % holds
+        front_copy(step, slot).wait()
+
+        @pl.when(step >= holds)
+        def _():
+            out_copy(step - holds, hold).wait()
+
+        lead = solved[...].astype(BF16)
+        for n in range(local_cols // span):
+            at = slice(n * span, (n + 1) * span)
+            update = dot(lead, flipped[:, at])
+            product = dot(own, kids[:, at])
+            group_all = tile_values(group_of, first_tile + n * (span // TS), span // TS)
+            kid_all = tile_values(kid_of, first_tile + n * (span // TS), span // TS)
+            for i in range(subs):
+                part = slice(i * TS, (i + 1) * TS)
+                outs[hold, part, at] = (
+                    jnp.where(group_all == group_of[my_tile + i], fronts[slot, part, at], 0.0)
+                    + jnp.where(kid_all == kid_of[my_tile + i], product[part], 0.0)
+                    + update[part]
+                )
+        for q in range(fan):
+            outs[hold, :, q * local_rows : q * local_rows + held] = jnp.zeros((block_rows, held), F32)
+
+        @pl.when(step == 0)
+        def _():
+            outs[hold, :held, :] = jnp.zeros((held, local_cols), F32)
+
+        out_copy(step, hold).start()
+
+        @pl.when(step + ins < steps)
+        def _():
+            front_copy(step + ins, slot).start()
+
+        return carry
+
+    lax.fori_loop(0, steps, work_rows, 0)
+    for i in range(max(0, steps - holds), steps):
+        out_copy(i, i % holds).wait()
 
 
 def params():
@@ -391,9 +460,11 @@
     halves = [row_strip[None, : local_rows // 2], row_strip[None, local_rows // 2 :]]
     masks = [[0], [0]]
     for h in range(2):
-        for step in orders[h][:-1]:
+        for step in orders[h][:-2]:
             halves[h] = jnp.concatenate([halves[h], swapped(halves[h], "col", step)], axis=0)
             masks[h] = masks[h] + [m ^ step for m in masks[h]]
+    others = [swapped(halves[h], "col", orders[h][-2]) for h in range(2)]
+    masks = [masks[h] + [m ^ orders[h][-2] for m in masks[h]] for h in range(2)]
     gathered = lax.all_gather(flipped, "row", axis=0)
     col_strip, *packets = lax.optimization_barrier((front_entries[:held].astype(BF16), *packets))
     col_strips = lax.all_gather(col_strip, "row", axis=0)
@@ -450,8 +521,9 @@
         name="first_pivots",
     )(place, group_of, kid_of, near, far)
 
-    rest, *arrived = lax.optimization_barrier((rest, *kid_parts, *halves))
-    kid_parts, halves = arrived[:cols], arrived[cols:]
+    rest, *arrived = lax.optimization_barrier((rest, *halves, *others))
+    halves = [jnp.concatenate([arrived[h], arrived[2 + h]], axis=0) for h in range(2)]
+    *halves, rest, kid_parts = lax.optimization_barrier((*halves, rest, kid_parts))
     near_kids = jnp.concatenate([part[slice_cols:] for part in kid_parts], axis=0)
     rest, near_kids = lax.optimization_barrier((rest, near_kids))
     far_kids = swapped(near_kids, "row", 1)
@@ -468,45 +540,46 @@
         name="second_pivots",
     )(rest)
 
-    block_rows = min(256, local_rows // 2)
-    per_half = local_rows // 2 // block_rows
-    wide = min(1024, local_cols)
-    piece = (cols // 2, block_rows, fan * held)
+    block_rows = min(256, local_rows)
+    wide = min(512, local_cols)
+    ins, holds = min(4, local_rows // block_rows), min(3, local_rows // block_rows)
     schur_block, factor_panels = pl.pallas_call(
         functools.partial(
             schur_kernel,
-            (rows, cols, fan, share, held, slice_cols, block_rows, local_rows, local_cols, tiles),
+            (rows, cols, fan, share, held, slice_cols, block_rows, local_rows, local_cols, tiles, wide),
             masks,
         ),
-        grid=(2 * per_half,),
         out_shape=[
             jax.ShapeDtypeStruct((local_rows, local_cols), F32),
             jax.ShapeDtypeStruct((local_rows, NP * PW // cols), BF16),
         ],
-        in_specs=[smem_spec()] * 3
-        + [pl.BlockSpec((block_rows, local_cols), lambda i: (i, 0))]
-        + [whole_spec()] * 17
-        + [pl.BlockSpec((2 * slice_cols, block_rows), lambda i: (0, i))] * cols
-        + [pl.BlockSpec(piece, lambda i: (0, jnp.minimum(i, per_half - 1), 0))] * 2
-        + [pl.BlockSpec(piece, lambda i: (0, jnp.maximum(i - per_half, 0), 0))] * 2,
-        out_specs=[
-            pl.BlockSpec((block_rows, local_cols), lambda i: (i, 0)),
-            pl.BlockSpec((block_rows, NP * PW // cols), lambda i: (i, 0)),
-        ],
+        in_specs=[smem_spec()] * 3 + [whole_spec()] * 14 + [any_spec()] * (8 + cols),
+        out_specs=[any_spec(), whole_spec()],
         scratch_shapes=[
+            pltpu.VMEM((ins, block_rows, local_cols), F32),
+            pltpu.VMEM((holds, block_rows, local_cols), F32),
+            pltpu.VMEM((rows, held, local_cols), BF16),
+            pltpu.VMEM((kid_cols, local_cols), BF16),
+            pltpu.VMEM((kid_cols, local_rows), BF16),
+            pltpu.VMEM((cols, local_rows, fan * held), F32),
             pltpu.VMEM((NPIV, local_cols), BF16),
-            pltpu.VMEM((kid_cols, local_cols), BF16),
             pltpu.VMEM((NPIV, wide), F32),
             pltpu.VMEM((block_rows, NPIV), F32),
-            pltpu.VMEM((cols, block_rows, fan * held), F32),
+            pltpu.SemaphoreType.DMA((ins,)),
+            pltpu.SemaphoreType.DMA((holds,)),
+            pltpu.SemaphoreType.DMA((local_cols // wide,)),
+            pltpu.SemaphoreType.DMA((fan,)),
+            pltpu.SemaphoreType.DMA((cols,)),
+            pltpu.SemaphoreType.DMA((2 * cols,)),
         ],
         compiler_params=params(),
         cost_estimate=pl.CostEstimate(flops=3 * 10**10, bytes_accessed=9 * 10**7, transcendentals=0),
         name="schur_update",
     )(
-        place, group_of, kid_of, front_entries, col_strips, near_kids, far_kids,
+        place, group_of, kid_of,
         piv, piv_t, lower1, lower2, inv1_hi, inv1_lo, inv2_hi, inv2_lo, link,
-        inv1_t_hi, inv1_t_lo, inv2_t_hi, inv2_t_lo, link_t, *kid_parts,
+        inv1_t_hi, inv1_t_lo, inv2_t_hi, inv2_t_lo, link_t,
+        front_entries, col_strips, near_kids, far_kids, *kid_parts,
         halves[0], others[0], halves[1], others[1],
     )
     return (factor_panels, schur_block)

time: 162 us -> 150 us (0.926)
  waiting for transfers between devices: 32.6 us -> 20.5 us
  other arithmetic: 6.05 us -> 4.07 us
  local copies, waits for them, and re-layouts: 9.54 us -> 11.5 us
    ppermute x15, waiting for transfers between devices: 31.9 us -> 19.1 us  [swapped(): lax.ppermute(value, axis, [(i, i ^ mask) for i in range(lax.axis_size(axi...]
  transfers between devices with their start and end apart: 17 -> 17, of which waited for: 7 -> 8; matrix products, arithmetic and copies ran while one was open for 9% -> 9% of each run, Pallas kernels for 25% -> 27%
where the time goes in v1:
time: 150 us
  Pallas kernels  80.1 us (53%)
  waiting for transfers between devices  20.5 us (14%)
  starting transfers between devices  19.5 us (13%)
  between operations  14.3 us (10%)
  local copies, waits for them, and re-layouts  11.5 us (8%)
  other arithmetic  4.07 us (3%)
    pallas_call x1, Pallas kernels, local(): pl.pallas_call(functools.partial(schur_kernel, (rows, cols, fan, share, h...  40.2 us
    pallas_call x1, Pallas kernels, local(): pl.pallas_call(functools.partial(first_kernel, (cols, fan, share, held, t...  19.4 us
    ppermute x15, starting transfers between devices, swapped(): lax.ppermute(value, axis, [(i, i ^ mask) for i in range(lax.axis_size(axi...  19.4 us
    ppermute x15, waiting for transfers between devices, swapped(): lax.ppermute(value, axis, [(i, i ^ mask) for i in range(lax.axis_size(axi...  19.1 us
    pallas_call x1, Pallas kernels, local(): pl.pallas_call(second_kernel, out_shape=[jax.ShapeDtypeStruct((PW, PW), F...  16.8 us
    pallas_call x1, Pallas kernels, local(): pl.pallas_call(functools.partial(place_kernel, (cols, fan, tiles, slice_c...  3.68 us
  transfers between devices with their start and end apart: 17, of which 8 were waited for; matrix products, arithmetic and copies ran while one was open for 9% of the time, Pallas kernels for 27%

profile of v1, /device:TPU:0, one launch (start us, length us, event | category | flops | bytes accessed | tf_op | source)
XLA Modules:
  0.0 149.9 jit_solution(7888005261047173468)
XLA Ops:
  7.2 0.7 all-gather.5.cloned.1.call-update
  8.0 1.0 copy.6
  8.9 0.7 broadcast_compare_fusion
  10.1 0.9 fusion.2
  11.1 5.1 %collective-permute-start.2 = (f32[128,128]{1,0:T(8,128)S(1)}, f32[128,128]{1,0:T(8,128)S(1)}, u32[]{:S(2)}, u32[]{:S(2)}) collective-permute-start(f32[128,128]{1,0:T(8,128)S(1)} %maximum_maximum_fusion), channel_id=1, source_target_pairs={{0,24},{4,28},{8,16},{12,20},{16,8},{20,12},{24,0},{28,4},{1,25},{... | collective-permute-start | bytes 196616 | tf_op jit(solution)/shard_map/ppermute | solution.py:40
  16.9 2.1 %slice.170 = bf16[64,4096]{1,0:T(8,128)(2,1)} slice(f32[2048,4096]{1,0:T(8,128)} %refs_0_.1), slice={[0:64], [0:4096]} | slice | bytes 1048576 | tf_op jit(solution)/shard_map/slice | solution.py:469
  19.0 2.9 %collective-permute-done.1 = f32[128,128]{1,0:T(8,128)S(1)} collective-permute-done((f32[128,128]{1,0:T(8,128)S(1)}, f32[128,128]{1,0:T(8,128)S(1)}, u32[]{:S(2)}, u32[]{:S(2)}) %collective-permute-start.1) | collective-permute-done | bytes 65568 | tf_op jit(solution)/shard_map/ppermute | solution.py:40
  22.4 1.6 %collective-permute-start.4 = (f32[4,96,128]{2,1,0:T(8,128)S(1)}, f32[4,96,128]{2,1,0:T(8,128)S(1)}, u32[]{:S(2)}, u32[]{:S(2)}) collective-permute-start(f32[4,96,128]{2,1,0:T(8,128)S(1)} %get-tuple-element.107), channel_id=1, source_target_pairs={{0,2},{1,3},{2,0},{3,1},{4,6},{5,7},{6,4},{7,5},{8,10},{9,11},{10,... | collective-permute-start | bytes 589832 | tf_op jit(solution)/shard_map/ppermute | solution.py:40
  24.0 1.5 collective-permute-start.3
  25.9 2.9 %fusion.1 = (f32[2048,32]{1,0:T(8,128)S(1)}, f32[2048,32]{1,0:T(8,128)S(1)}, f32[2048,32]{1,0:T(8,128)S(1)}, f32[2048,32]{1,0:T(8,128)S(1)}) fusion(f32[2048,4096]{1,0:T(8,128)} %refs_0_.1), kind=kLoop, calls=%fused_computation.27 | loop fusion | bytes 2097152 | tf_op jit(solution)/shard_map/slice | solution.py:452
  29.3 2.5 %collective-permute-done.3 = f32[4,96,128]{2,1,0:T(8,128)S(1)} collective-permute-done((f32[4,96,128]{2,1,0:T(8,128)S(1)}, f32[4,96,128]{2,1,0:T(8,128)S(1)}, u32[]{:S(2)}, u32[]{:S(2)}) %collective-permute-start.3) | collective-permute-done | bytes 196640 | tf_op jit(solution)/shard_map/ppermute | solution.py:40
  31.8 2.6 %collective-permute-done.5 = f32[4,96,128]{2,1,0:T(8,128)S(1)} collective-permute-done((f32[4,96,128]{2,1,0:T(8,128)S(1)}, f32[4,96,128]{2,1,0:T(8,128)S(1)}, u32[]{:S(2)}, u32[]{:S(2)}) %collective-permute-start.5) | collective-permute-done | bytes 196640 | tf_op jit(solution)/shard_map/ppermute | solution.py:40
  34.5 0.9 pad_maximum_fusion
  35.5 1.7 %collective-permute-start.8 = (f32[1,1024,128]{2,1,0:T(8,128)S(1)}, f32[1,1024,128]{2,1,0:T(8,128)S(1)}, u32[]{:S(2)}, u32[]{:S(2)}) collective-permute-start(f32[1,1024,128]{2,1,0:T(8,128)S(1)} %get-tuple-element.64), channel_id=1, source_target_pairs={{0,2},{1,3},{2,0},{3,1},{4,6},{5,7},{6,4},{7,5},{8,10},{9,11},{10,... | collective-permute-start | bytes 1572872 | tf_op jit(solution)/shard_map/ppermute | solution.py:40
  37.2 1.5 collective-permute-start.7
  39.4 0.6 pad_add_fusion.place
  40.7 0.7 all-gather.5.cloned.1.call-done
  41.4 3.7 %place_tiles.1 = (bf16[128,2048]{1,0:T(8,128)(2,1)}, bf16[128,2048]{1,0:T(8,128)(2,1)}, bf16[128,2048]{1,0:T(8,128)(2,1)}, bf16[128,2048]{1,0:T(8,128)(2,1)}) custom-call(s32[2]{0:T(128)} %pad_add_fusion.place, s32[128]{0:T(128)} %copy-done.9, bf16[8,64,2048]{2,1,0:T(8,128)(2,1)} %bitcast.24), custom_call_target="tpu_custom_call" | custom-call | bytes 8388608 | tf_op jit(solution)/shard_map/place_tiles/pallas_call | solution.py:491
  45.1 1.4 collective-permute-start.9
  46.5 1.6 %collective-permute-start.10 = (bf16[128,2048]{1,0:T(8,128)(2,1)}, bf16[128,2048]{1,0:T(8,128)(2,1)}, u32[]{:S(2)}, u32[]{:S(2)}) collective-permute-start(bf16[128,2048]{1,0:T(8,128)(2,1)} %get-tuple-element.69), channel_id=1, source_target_pairs={{0,2},{1,3},{2,0},{3,1},{4,6},{5,7},{6,4},{7,5},{8,10},{9,11},{10,... | collective-permute-start | bytes 1572872 | tf_op jit(solution)/shard_map/ppermute | solution.py:40
  48.6 19.4 %first_pivots.1 = (f32[512,256]{1,0:T(8,128)}, bf16[256,256]{1,0:T(8,128)(2,1)}, bf16[256,256]{1,0:T(8,128)(2,1)}, bf16[256,256]{1,0:T(8,128)(2,1)}, bf16[256,25...) custom-call(s32[2]{0:T(128)} %pad_add_fusion.place, ...), custom_call_target="tpu_custom_call" | custom-call | flops 20000000000 | bytes 50000000 | tf_op jit(solution)/shard_map/first_pivots/pallas_call | solution.py:503
  68.0 0.8 copy-done.4
  68.9 1.0 copy-done.5
  69.9 3.7 %collective-permute-done.11.refs_7_ = bf16[128,2048]{1,0:T(8,128)(2,1)} collective-permute-done((bf16[128,2048]{1,0:T(8,128)(2,1)}, bf16[128,2048]{1,0:T(8,128)(2,1)}, u32[]{:S(2)}, u32[]{:S(2)}) %collective-permute-start.11) | collective-permute-done | bytes 524320 | tf_op jit(solution)/shard_map/ppermute | solution.py:40
  73.7 1.0 slice.143
  74.7 1.0 slice.144
  75.8 1.7 %collective-permute-start.13 = (f32[2,1024,128]{2,1,0:T(8,128)S(1)}, f32[2,1024,128]{2,1,0:T(8,128)}, u32[]{:S(2)}, u32[]{:S(2)}) collective-permute-start(f32[2,1024,128]{2,1,0:T(8,128)S(1)} %pad_maximum_fusion.1.refs_8_), channel_id=1, source_target_pairs={{0,2},{1,3},{2,0},{3,1},{4,6},{5,7},{6,4},{7,5},{8,10},{9,11},{10,... | collective-permute-start | bytes 3145736 | tf_op jit(solution)/shard_map/ppermute | solution.py:40
  77.6 1.5 collective-permute-start.14
  79.1 16.8 %second_pivots.1 = (f32[256,256]{1,0:T(8,128)}, bf16[256,256]{1,0:T(8,128)(2,1)}, bf16[256,256]{1,0:T(8,128)(2,1)}, bf16[256,256]{1,0:T(8,128)(2,1)}, bf16[256,256]{1,0:T(8,128)(2,1)}) custom-call(f32[256,256]{1,0:T(8,128)} %get-tuple-element.76.rest), custom_call_target="tpu_custom_call" | custom-call | flops 20000000000 | bytes 50000000 | tf_op jit(solution)/shard_map/second_pivots/pallas_call | solution.py:532
  95.9 5.6 %collective-permute-done.13.refs_9_ = f32[2,1024,128]{2,1,0:T(8,128)} collective-permute-done((f32[2,1024,128]{2,1,0:T(8,128)S(1)}, f32[2,1024,128]{2,1,0:T(8,128)}, u32[]{:S(2)}, u32[]{:S(2)}) %collective-permute-start.13) | collective-permute-done | bytes 1048608 | tf_op jit(solution)/shard_map/ppermute | solution.py:40
  101.5 1.4 collective-permute-done.14.refs_11_
  102.9 40.2 %schur_update.1 = (f32[2048,4096]{1,0:T(8,128)}, bf16[2048,128]{1,0:T(8,128)(2,1)}) custom-call(s32[2]{0:T(128)} %pad_add_fusion.place, f32[128]{0:T(128)} %convert_element_type.19.group_of, f32[128]{0:T(128)} %compare_convert_fusion.kid_of, bf16[512,256]{1,0:T(8,128)(2,1)} %get-tuple-element.58.piv, bf16[256,512]{1,0:T(8,128)(2,1)} %get-tuple-element.59.piv_t, ...), custom_call_target="tpu_custom_call" | custom-call | flops 30000001024 | bytes 90000000 | tf_op jit(solution)/shard_map/schur_update/pallas_call | solution.py:546
  (67 shorter events, 5.0 us)
Async XLA Ops:
  7.2 34.2 %all-gather.5.cloned.1.call-start = ((), (), s32[]{:S(2)}) async-start(), calls=%async_computation | async-start | bytes 2359296 | tf_op jit(solution)/shard_map/all_gather | solution.py:468
  7.9 95.0 %all-gather.7.cloned.1.call-start = ((), (), s32[]{:S(2)}) async-start(), calls=%async_computation.1 | async-start | bytes 4718592 | tf_op jit(solution)/shard_map/all_gather | solution.py:470
  11.1 7.8 %collective-permute-start.2 = (f32[128,128]{1,0:T(8,128)S(1)}, f32[128,128]{1,0:T(8,128)S(1)}, u32[]{:S(2)}, u32[]{:S(2)}) collective-permute-start(f32[128,128]{1,0:T(8,128)S(1)} %maximum_maximum_fusion), channel_id=1, source_target_pairs={{0,24},{4,28},{8,16},{12,20},{16,8},{20,12},{24,0},{28,4},{1,25},{... | collective-permute-start | bytes 196616 | tf_op jit(solution)/shard_map/ppermute | solution.py:40
  16.2 5.6 %collective-permute-start.1 = (f32[128,128]{1,0:T(8,128)S(1)}, f32[128,128]{1,0:T(8,128)S(1)}, u32[]{:S(2)}, u32[]{:S(2)}) collective-permute-start(f32[128,128]{1,0:T(8,128)S(1)} %maximum_maximum_fusion), channel_id=1, source_target_pairs={{0,16},{4,20},{8,24},{12,28},{16,0},{20,4},{24,8},{28,12},{1,17},{... | collective-permute-start | bytes 196616 | tf_op jit(solution)/shard_map/ppermute | solution.py:40
  16.2 5.6 %collective-permute-start = (f32[128,128]{1,0:T(8,128)S(1)}, f32[128,128]{1,0:T(8,128)S(1)}, u32[]{:S(2)}, u32[]{:S(2)}) collective-permute-start(f32[128,128]{1,0:T(8,128)S(1)} %maximum_maximum_fusion), channel_id=1, source_target_pairs={{0,8},{4,12},{8,0},{12,4},{16,24},{20,28},{24,16},{28,20},{1,9},{5... | collective-permute-start | bytes 196616 | tf_op jit(solution)/shard_map/ppermute | solution.py:40
  22.4 6.9 %collective-permute-start.4 = (f32[4,96,128]{2,1,0:T(8,128)S(1)}, f32[4,96,128]{2,1,0:T(8,128)S(1)}, u32[]{:S(2)}, u32[]{:S(2)}) collective-permute-start(f32[4,96,128]{2,1,0:T(8,128)S(1)} %get-tuple-element.107), channel_id=1, source_target_pairs={{0,2},{1,3},{2,0},{3,1},{4,6},{5,7},{6,4},{7,5},{8,10},{9,11},{10,... | collective-permute-start | bytes 589832 | tf_op jit(solution)/shard_map/ppermute | solution.py:40
  24.0 7.8 %collective-permute-start.3 = (f32[4,96,128]{2,1,0:T(8,128)S(1)}, f32[4,96,128]{2,1,0:T(8,128)S(1)}, u32[]{:S(2)}, u32[]{:S(2)}) collective-permute-start(f32[4,96,128]{2,1,0:T(8,128)S(1)} %get-tuple-element.107), channel_id=1, source_target_pairs={{0,1},{1,0},{2,3},{3,2},{4,5},{5,4},{6,7},{7,6},{8,9},{9,8},{10,11... | collective-permute-start | bytes 589832 | tf_op jit(solution)/shard_map/ppermute | solution.py:40
  25.5 8.9 %collective-permute-start.5 = (f32[4,96,128]{2,1,0:T(8,128)S(1)}, f32[4,96,128]{2,1,0:T(8,128)S(1)}, u32[]{:S(2)}, u32[]{:S(2)}) collective-permute-start(f32[4,96,128]{2,1,0:T(8,128)S(1)} %get-tuple-element.107), channel_id=1, source_target_pairs={{0,3},{1,2},{2,1},{3,0},{4,7},{5,6},{6,5},{7,4},{8,11},{9,10},{10,... | collective-permute-start | bytes 589832 | tf_op jit(solution)/shard_map/ppermute | solution.py:40
  34.4 1.0 copy-start.3
  34.4 10.7 %collective-permute-start.6 = (f32[4,4,96,128]{3,2,1,0:T(8,128)S(1)}, f32[4,4,96,128]{3,2,1,0:T(8,128)}, u32[]{:S(2)}, u32[]{:S(2)}) collective-permute-start(f32[4,4,96,128]{3,2,1,0:T(8,128)S(1)} %pad_maximum_fusion.4.near), channel_id=1, source_target_pairs={{0,4},{4,0},{8,12},{12,8},{16,20},{20,16},{24,28},{28,24},{1,5},{5... | collective-permute-start | bytes 2359304 | tf_op jit(solution)/shard_map/ppermute | solution.py:40
  35.4 3.3 %copy-start.10 = (s32[32]{0:T(128)S(1)}, s32[32]{0:T(128)}, u32[]{:S(2)}) copy-start(s32[32]{0:T(128)} %param.5) | copy-start | bytes 388
  35.4 4.7 %copy-start.8 = (s32[128]{0:T(128)S(1)}, s32[128]{0:T(128)}, u32[]{:S(2)}) copy-start(s32[128]{0:T(128)} %param.7) | copy-start | bytes 1540
  35.5 32.5 %collective-permute-start.8 = (f32[1,1024,128]{2,1,0:T(8,128)S(1)}, f32[1,1024,128]{2,1,0:T(8,128)S(1)}, u32[]{:S(2)}, u32[]{:S(2)}) collective-permute-start(f32[1,1024,128]{2,1,0:T(8,128)S(1)} %get-tuple-element.64), channel_id=1, source_target_pairs={{0,2},{1,3},{2,0},{3,1},{4,6},{5,7},{6,4},{7,5},{8,10},{9,11},{10,... | collective-permute-start | bytes 1572872 | tf_op jit(solution)/shard_map/ppermute | solution.py:40
  37.2 30.8 %collective-permute-start.7 = (f32[1,1024,128]{2,1,0:T(8,128)S(1)}, f32[1,1024,128]{2,1,0:T(8,128)S(1)}, u32[]{:S(2)}, u32[]{:S(2)}) collective-permute-start(f32[1,1024,128]{2,1,0:T(8,128)S(1)} %get-tuple-element.62), channel_id=1, source_target_pairs={{0,1},{1,0},{2,3},{3,2},{4,5},{5,4},{6,7},{7,6},{8,9},{9,8},{10,11... | collective-permute-start | bytes 1572872 | tf_op jit(solution)/shard_map/ppermute | solution.py:40
  40.2 1.2 copy-start.9
  45.1 24.8 %collective-permute-start.9 = (bf16[128,2048]{1,0:T(8,128)(2,1)}, bf16[128,2048]{1,0:T(8,128)(2,1)S(1)}, u32[]{:S(2)}, u32[]{:S(2)}) collective-permute-start(bf16[128,2048]{1,0:T(8,128)(2,1)} %get-tuple-element.68), channel_id=1, source_target_pairs={{0,1},{1,0},{2,3},{3,2},{4,5},{5,4},{6,7},{7,6},{8,9},{9,8},{10,11... | collective-permute-start | bytes 1572872 | tf_op jit(solution)/shard_map/ppermute | solution.py:40
  46.5 23.4 %collective-permute-start.10 = (bf16[128,2048]{1,0:T(8,128)(2,1)}, bf16[128,2048]{1,0:T(8,128)(2,1)}, u32[]{:S(2)}, u32[]{:S(2)}) collective-permute-start(bf16[128,2048]{1,0:T(8,128)(2,1)} %get-tuple-element.69), channel_id=1, source_target_pairs={{0,2},{1,3},{2,0},{3,1},{4,6},{5,7},{6,4},{7,5},{8,10},{9,11},{10,... | collective-permute-start | bytes 1572872 | tf_op jit(solution)/shard_map/ppermute | solution.py:40
  48.1 25.6 %collective-permute-start.11 = (bf16[128,2048]{1,0:T(8,128)(2,1)}, bf16[128,2048]{1,0:T(8,128)(2,1)}, u32[]{:S(2)}, u32[]{:S(2)}) collective-permute-start(bf16[128,2048]{1,0:T(8,128)(2,1)} %get-tuple-element.70), channel_id=1, source_target_pairs={{0,3},{1,2},{2,1},{3,0},{4,7},{5,6},{6,5},{7,4},{8,11},{9,10},{10,... | collective-permute-start | bytes 1572872 | tf_op jit(solution)/shard_map/ppermute | solution.py:40
  68.0 0.8 copy-start.4
  68.8 1.0 copy-start.5
  68.8 4.9 %copy-start.6 = (bf16[128,2048]{1,0:T(8,128)(2,1)S(1)}, bf16[128,2048]{1,0:T(8,128)(2,1)}, u32[]{:S(2)}) copy-start(bf16[128,2048]{1,0:T(8,128)(2,1)} %get-tuple-element.72.refs_4_) | copy-start | bytes 1572868
  69.8 6.0 %copy-start = (f32[2,1024,128]{2,1,0:T(8,128)}, f32[2,1024,128]{2,1,0:T(8,128)S(1)}, u32[]{:S(2)}) copy-start(f32[2,1024,128]{2,1,0:T(8,128)S(1)} %pad_maximum_fusion.1.refs_8_) | copy-start | bytes 3145732
  69.9 7.7 %copy-start.1 = (f32[2,1024,128]{2,1,0:T(8,128)}, f32[2,1024,128]{2,1,0:T(8,128)S(1)}, u32[]{:S(2)}) copy-start(f32[2,1024,128]{2,1,0:T(8,128)S(1)} %pad_maximum_fusion.2.refs_10_) | copy-start | bytes 3145732
  69.9 4.8 %copy-start.7 = (bf16[128,2048]{1,0:T(8,128)(2,1)}, bf16[128,2048]{1,0:T(8,128)(2,1)S(1)}, u32[]{:S(2)}) copy-start(bf16[128,2048]{1,0:T(8,128)(2,1)S(1)} %collective-permute-done.9.refs_5_) | copy-start | bytes 1572868
  75.7 20.2 %copy-start.2 = (bf16[256,2048]{1,0:T(8,128)(2,1)}, bf16[256,2048]{1,0:T(8,128)(2,1)S(1)}, u32[]{:S(2)}) copy-start(bf16[256,2048]{1,0:T(8,128)(2,1)S(1)} %pad_maximum_fusion.3.refs_2_) | copy-start | bytes 3145732
  75.7 20.1 %collective-permute-start.12 = (bf16[256,2048]{1,0:T(8,128)(2,1)S(1)}, bf16[256,2048]{1,0:T(8,128)(2,1)}, u32[]{:S(2)}, u32[]{:S(2)}) collective-permute-start(bf16[256,2048]{1,0:T(8,128)(2,1)S(1)} %pad_maximum_fusion.3.refs_2_), channel_id=1, source_target_pairs={{0,4},{4,0},{8,12},{12,8},{16,20},{20,16},{24,28},{28,24},{1,5},{5... | collective-permute-start | bytes 3145736 | tf_op jit(solution)/shard_map/ppermute | solution.py:40
  75.8 25.7 %collective-permute-start.13 = (f32[2,1024,128]{2,1,0:T(8,128)S(1)}, f32[2,1024,128]{2,1,0:T(8,128)}, u32[]{:S(2)}, u32[]{:S(2)}) collective-permute-start(f32[2,1024,128]{2,1,0:T(8,128)S(1)} %pad_maximum_fusion.1.refs_8_), channel_id=1, source_target_pairs={{0,2},{1,3},{2,0},{3,1},{4,6},{5,7},{6,4},{7,5},{8,10},{9,11},{10,... | collective-permute-start | bytes 3145736 | tf_op jit(solution)/shard_map/ppermute | solution.py:40
  77.6 25.3 %collective-permute-start.14 = (f32[2,1024,128]{2,1,0:T(8,128)S(1)}, f32[2,1024,128]{2,1,0:T(8,128)}, u32[]{:S(2)}, u32[]{:S(2)}) collective-permute-start(f32[2,1024,128]{2,1,0:T(8,128)S(1)} %pad_maximum_fusion.2.refs_10_), channel_id=1, source_target_pairs={{0,1},{1,0},{2,3},{3,2},{4,5},{5,4},{6,7},{7,6},{8,9},{9,8},{10,11... | collective-permute-start | bytes 3145736 | tf_op jit(solution)/shard_map/ppermute | solution.py:40
Sparse Core Ops, SparseCore 0:
  9.6 31.7 all-gather.4
  43.6 46.9 all-gather.6

commit v2 on v1

--- a/solution.py
+++ b/solution.py
@@ -64,25 +64,40 @@
         base = 8 * (k // 8)
         cols.append(jnp.broadcast_to(block[base:, k : k + 1], (BLK - base, 128)))
     scale = [jnp.ones((8, 128), F32) for _ in range(groups)]
-    for j in range(BLK):
+
+    def inverse_root(value):
+        root = lax.rsqrt(value)
+        return root * (1.5 - 0.5 * value * root * root)
+
+    for j in range(0, BLK, 2):
         g0 = j // 8
         base = 8 * g0
-        column = cols[j]
-        pivot = column[j - base : j - base + 1]
-        root = lax.rsqrt(pivot)
-        root = root * (1.5 - 0.5 * pivot * root * root)
-        factor = jnp.where(row[base:] > j, column * (root * root), 0.0)
-        lead = work[g0][j - base : j - base + 1]
+        one, two = cols[j], cols[j + 1]
+        first, cross, last = one[j - base : j - base + 1], one[j - base + 1 : j - base + 2], two[j - base + 1 : j - base + 2]
+        volume = first * last - cross * cross
+        root = inverse_root(volume)
+        inverse = root * root
+        below = row[base:] > j + 1
+        lead_one = jnp.where(below, last * one - cross * two, 0.0) * inverse
+        lead_two = jnp.where(below, first * two - cross * one, 0.0) * inverse
+        row_one, row_two = work[g0][j - base : j - base + 1], work[g0][j - base + 1 : j - base + 2]
+        for k in range(j + 2, BLK):
+            skip = 8 * (k // 8 - g0)
+            cols[k] = cols[k] - (
+                lead_one[skip:] * one[k - base : k - base + 1] + lead_two[skip:] * two[k - base : k - base + 1]
+            )
         for g in range(g0, groups):
-            work[g] = work[g] - factor[8 * (g - g0) : 8 * (g - g0) + 8] * lead
-        for k in range(j + 1, BLK):
-            skip = 8 * (k // 8 - g0)
-            cols[k] = cols[k] - factor[skip:] * column[k - base : k - base + 1]
-        scale[g0] = jnp.where(row8 == j - base, root, scale[g0])
+            part = slice(8 * (g - g0), 8 * (g - g0) + 8)
+            work[g] = work[g] - (lead_one[part] * row_one + lead_two[part] * row_two)
+        first_root = inverse_root(first)
+        ratio = cross * (first_root * first_root)
+        work[g0] = work[g0] - jnp.where(row8 == j - base + 1, ratio, 0.0) * row_one
+        scale[g0] = jnp.where(row8 == j - base, first_root, scale[g0])
+        scale[g0] = jnp.where(row8 == j - base + 1, first * first_root * root, scale[g0])
     return jnp.concatenate([work[g] * scale[g] for g in range(groups)], axis=0)
 
 
-def factor_panel(work):
+def factor_panel(work, start, stop):
     per_tile = 128 // BLK
     row = lax.broadcasted_iota(jnp.int32, (PW, BLK), 0)
     lane = lax.broadcasted_iota(jnp.int32, (BLK, 128), 1)
@@ -102,7 +117,22 @@
         work[pl.ds(low, BLK), :] = upper
         return carry
 
-    lax.fori_loop(0, PW // BLK, step, 0)
+    lax.fori_loop(start, stop, step, 0)
+
+
+def diagonals(value):
+    row = lax.broadcasted_iota(jnp.int32, (PW, PW), 0)
+    col = lax.broadcasted_iota(jnp.int32, (PW, PW), 1)
+    kept = jnp.where(row == col, value, 0.0)
+    return jnp.sum(kept, axis=1, keepdims=True), jnp.sum(kept, axis=0, keepdims=True)
+
+
+def start_panel(work, diag_col, diag_row, value):
+    by_row, by_col = diagonals(value)
+    diag_col[...] = jnp.broadcast_to(by_row, (PW, 128))
+    diag_row[...] = jnp.broadcast_to(by_col, (8, PW))
+    work[:, :PW] = value / jnp.sqrt(by_row) / jnp.sqrt(by_col)
+    work[:, PW:] = unit()
 
 
 def pivot_values(table, stride, share, along_rows):
@@ -118,11 +148,11 @@
     return jnp.concatenate([jnp.full((1, TS), table[start + i], F32) for i in range(count)], axis=1)
 
 
-def finish_panel(work, lower, inv_hi, inv_lo, inv_t_hi, inv_t_lo):
+def finish_panel(work, diag_col, diag_row, lower, inv_hi, inv_lo, inv_t_hi, inv_t_lo):
     row = lax.broadcasted_iota(jnp.int32, (PW, PW), 0)
     col = lax.broadcasted_iota(jnp.int32, (PW, PW), 1)
-    lower[:PW, :] = jnp.where(col <= row, work[:, :PW].T, 0.0)
-    inverse = work[:, PW:]
+    lower[:PW, :] = jnp.where(col <= row, work[:, :PW].T, 0.0) * jnp.sqrt(diag_col[:, :1])
+    inverse = work[:, PW:] / jnp.sqrt(diag_row[:1, :])
     inv_hi[...], inv_lo[...] = split(inverse)
     inv_t_hi[...], inv_t_lo[...] = split(inverse.T)
     return inverse
@@ -134,9 +164,8 @@
     return jnp.where(row == col, 1.0, 0.0)
 
 
-def first_kernel(sizes, place, group_of, kid_of, near, far,
-                 lower, inv_hi, inv_lo, inv_t_hi, inv_t_lo, link_out, link_t, rest, piv_t, piv,
-                 pile, wide, work):
+def open_kernel(sizes, place, group_of, kid_of, near, far,
+                work, diag_col, diag_row, low_rows, piv_t, piv, pile, wide):
     cols, fan, share, held, tiles = sizes
     my_row, my_col = place[0], place[1]
     my_q, my_a = my_row % fan, my_row // fan
@@ -164,22 +193,27 @@
     same_group = pivot_values(group_of, tiles, share, True) == pivot_values(group_of, tiles, share, False)
     same_kid = pivot_values(kid_of, tiles, share, True) == pivot_values(kid_of, tiles, share, False)
     pile[...] = jnp.where(same_group, pile[...], 0.0) + jnp.where(same_kid, product, 0.0)
-    work[:, :PW] = pile[:PW, :PW]
-    work[:, PW:] = unit()
-    factor_panel(work)
-    inverse = finish_panel(work, lower, inv_hi, inv_lo, inv_t_hi, inv_t_lo)
-    link = exact(pile[PW:, :PW], inverse, NT).astype(BF16)
+    low_rows[...] = pile[PW:, :]
+    start_panel(work, diag_col, diag_row, pile[:PW, :PW])
+    factor_panel(work, 0, PW // BLK // 2)
+
+
+def first_kernel(begun, diag_col, diag_row, low_rows,
+                 lower, inv_hi, inv_lo, inv_t_hi, inv_t_lo, link_out, link_t, rest, work):
+    work[...] = begun[...]
+    factor_panel(work, PW // BLK // 2, PW // BLK)
+    inverse = finish_panel(work, diag_col, diag_row, lower, inv_hi, inv_lo, inv_t_hi, inv_t_lo)
+    link = exact(low_rows[:, :PW], inverse, NT).astype(BF16)
     link_out[...] = link
     lower[PW:, :] = link.astype(F32)
     link_t[...] = link.astype(F32).T.astype(BF16)
-    rest[...] = pile[PW:, PW:] - dot(link, link, NT)
-
-
-def second_kernel(rest, lower, inv_hi, inv_lo, inv_t_hi, inv_t_lo, work):
-    work[:, :PW] = rest[...]
-    work[:, PW:] = unit()
-    factor_panel(work)
-    finish_panel(work, lower, inv_hi, inv_lo, inv_t_hi, inv_t_lo)
+    rest[...] = low_rows[:, PW:] - dot(link, link, NT)
+
+
+def second_kernel(rest, lower, inv_hi, inv_lo, inv_t_hi, inv_t_lo, work, diag_col, diag_row):
+    start_panel(work, diag_col, diag_row, rest[...])
+    factor_panel(work, 0, PW // BLK)
+    finish_panel(work, diag_col, diag_row, lower, inv_hi, inv_lo, inv_t_hi, inv_t_lo)
 
 
 def place_kernel(sizes, place, inverse_map, held, *outs):
@@ -199,23 +233,6 @@
     for d in range(cols):
         for i in range(tiles):
             outs[d][slice_cols:, i * TS : (i + 1) * TS] = fetch((my_col ^ d) * fan + my_q, i)
-
-
-def solve_rows(first, second, inv1_hi, inv1_lo, inv2_hi, inv2_lo, link):
-    high, low = split(first)
-    head = dot(high, inv1_hi) + dot(high, inv1_lo) + dot(low, inv1_hi)
-    high, low = split(second - dot(head.astype(BF16), link))
-    tail = dot(high, inv2_hi) + dot(high, inv2_lo) + dot(low, inv2_hi)
-    return head, tail
-
-
-def solve_cols(first, second, inv1_hi, inv1_lo, inv2_hi, inv2_lo, link):
-    def apply(inv_hi, inv_lo, value):
-        both = dot(jnp.concatenate([inv_hi, inv_lo], axis=0), value.astype(BF16))
-        return both[:PW] + both[PW:]
-
-    head = apply(inv1_hi, inv1_lo, first)
-    return head, apply(inv2_hi, inv2_lo, second - dot(link, head.astype(BF16)))
 
 
 def schur_kernel(sizes, masks, place, group_of, kid_of,
@@ -226,14 +243,14 @@
     sources = refs[4 : 4 + cols]
     halves = [refs[4 + cols : 6 + cols], refs[6 + cols : 8 + cols]]
     out, panel = refs[8 + cols : 10 + cols]
-    (fronts, outs, strips_in, kids, own_t, pieces, flipped, strip, solved,
+    (fronts, outs, strips_in, kids, own_t, pieces, flipped, strip, solved_even, solved_odd, own_even, own_odd,
      front_sems, out_sems, strip_sems, kid_sems, own_sems, piece_sems) = refs[10 + cols :]
     my_row, my_col = place[0], place[1]
     my_q = my_row % fan
     first_tile = my_col * fan * tiles
     steps = local_rows // block_rows
     chunks = local_cols // wide
-    ins, holds = fronts.shape[0], outs.shape[0]
+    depth = fronts.shape[0] // 2
     half_rows = local_rows // 2
 
     def rows_at(i):
@@ -287,37 +304,34 @@
     group_col = pivot_values(group_of, tiles, share, True)
     kid_col = pivot_values(kid_of, tiles, share, True)
 
-    def solve(n, carry):
-        strip_copy(n).wait()
-
-        @pl.when(n == 0)
-        def _():
-            for i in range(ins):
-                front_copy(i, i).start()
-
-        at = chunk_at(n)
+    def col_solve(n, pile):
+        at = slice(n * wide, (n + 1) * wide)
         for r in range(rows):
             piece = strips_in[r, :, at].astype(F32)
             for k in range(NP):
                 low = k * PW + r * share
-                strip[low : low + share, :] = piece[k * share : (k + 1) * share]
+                pile[low : low + share, :] = piece[k * share : (k + 1) * share]
         tile = first_tile + n * (wide // TS)
         group_all = tile_values(group_of, tile, wide // TS)
         kid_all = tile_values(kid_of, tile, wide // TS)
         product = dot(piv[...], kids[:, at])
-        full = jnp.where(group_col == group_all, strip[...], 0.0) + jnp.where(
+        yield
+        full = jnp.where(group_col == group_all, pile[...], 0.0) + jnp.where(
             kid_col == kid_all, product, 0.0
         )
-        head, tail = solve_cols(
-            full[:PW], full[PW:], inv1_hi[...], inv1_lo[...], inv2_hi[...], inv2_lo[...], link[...]
-        )
-        flipped[:PW, at] = (-head).astype(BF16)
-        flipped[PW:, at] = (-tail).astype(BF16)
-        return carry
-
-    lax.fori_loop(0, chunks, solve, 0)
-    for copy in own_copies + piece_copies:
-        copy.wait()
+        first, second = full[:PW].astype(BF16), full[PW:]
+        yield
+        both = dot(jnp.concatenate([inv1_hi[...], inv1_lo[...]], axis=0), first)
+        yield
+        head = (both[:PW] + both[PW:]).astype(BF16)
+        flipped[:PW, at] = -head
+        yield
+        second = (second - dot(link[...], head)).astype(BF16)
+        yield
+        both = dot(jnp.concatenate([inv2_hi[...], inv2_lo[...]], axis=0), second)
+        yield
+        flipped[PW:, at] = (-(both[:PW] + both[PW:])).astype(BF16)
+
     col_share = PW // cols
     subs = block_rows // TS
     per_tile = 128 // col_share
@@ -326,9 +340,11 @@
     kid_row = pivot_values(kid_of, tiles, share, False)
     lane = lax.broadcasted_iota(jnp.int32, (block_rows, 128), 1)
 
-    def work_rows(step, carry):
+    def row_solve(step, opening, own_ref, solved):
         own = own_t[:, rows_at(step)].astype(F32).T.astype(BF16)
+        own_ref[...] = own
         product = dot(own, piv_t[...])
+        yield
         entries = jnp.concatenate(
             [
                 pieces[c, rows_at(step), k * col_share : (k + 1) * col_share]
@@ -346,21 +362,21 @@
                 + jnp.where(kid_row == kid_of[my_tile + i], product[part], 0.0)
             )
         full = jnp.concatenate(parts, axis=0)
-        head, tail = solve_rows(
-            full[:, :PW], full[:, PW:],
-            inv1_t_hi[...], inv1_t_lo[...], inv2_t_hi[...], inv2_t_lo[...], link_t[...],
-        )
+        high, low = split(full[:, :PW])
+        yield
+        head = dot(high, inv1_t_hi[...]) + dot(high, inv1_t_lo[...]) + dot(low, inv1_t_hi[...])
         solved[:, :PW] = head
-        solved[:, PW:] = tail
-
-        @pl.when(step == 0)
-        def _():
+        yield
+        high, low = split(full[:, PW:] - dot(head.astype(BF16), link_t[...]))
+        yield
+        solved[:, PW:] = dot(high, inv2_t_hi[...]) + dot(high, inv2_t_lo[...]) + dot(low, inv2_t_hi[...])
+        yield
+        if opening:
             at = pl.multiple_of(my_row * share, share)
             solved[:share, :PW] = lower1[pl.ds(at, share), :]
             solved[:share, PW:] = jnp.zeros((share, PW), F32)
             solved[share : 2 * share, :PW] = lower1[pl.ds(PW + at, share), :]
             solved[share : 2 * share, PW:] = lower2[pl.ds(at, share), :]
-
         moved_out = jnp.zeros((block_rows, 128), F32)
         for k in range(NP):
             tile = pl.multiple_of(k * PW + (my_col // per_tile) * 128, 128)
@@ -369,45 +385,79 @@
             moved_out = jnp.where(lane // col_share == k, moved, moved_out)
         panel[rows_at(step), :] = moved_out[:, : NP * col_share].astype(BF16)
 
-        slot, hold = step % ins, step % holds
-        front_copy(step, slot).wait()
-
-        @pl.when(step >= holds)
-        def _():
-            out_copy(step - holds, hold).wait()
-
-        lead = solved[...].astype(BF16)
+    def update(step, slot, own_ref, solved):
+        lead, own = solved[...].astype(BF16), own_ref[...]
+        my_tile = my_row * tiles + step * subs
         for n in range(local_cols // span):
             at = slice(n * span, (n + 1) * span)
-            update = dot(lead, flipped[:, at])
+            change = dot(lead, flipped[:, at])
             product = dot(own, kids[:, at])
             group_all = tile_values(group_of, first_tile + n * (span // TS), span // TS)
             kid_all = tile_values(kid_of, first_tile + n * (span // TS), span // TS)
             for i in range(subs):
                 part = slice(i * TS, (i + 1) * TS)
-                outs[hold, part, at] = (
+                outs[slot, part, at] = (
                     jnp.where(group_all == group_of[my_tile + i], fronts[slot, part, at], 0.0)
                     + jnp.where(kid_all == kid_of[my_tile + i], product[part], 0.0)
-                    + update[part]
+                    + change[part]
                 )
-        for q in range(fan):
-            outs[hold, :, q * local_rows : q * local_rows + held] = jnp.zeros((block_rows, held), F32)
-
-        @pl.when(step == 0)
-        def _():
-            outs[hold, :held, :] = jnp.zeros((held, local_cols), F32)
-
-        out_copy(step, hold).start()
-
-        @pl.when(step + ins < steps)
-        def _():
-            front_copy(step + ins, slot).start()
+            yield
+
+    def together(*parts):
+        parts = list(parts)
+        while parts:
+            for part in list(parts):
+                try:
+                    next(part)
+                except StopIteration:
+                    parts.remove(part)
+
+    for n in range(0, chunks, 2):
+        pair = range(n, min(n + 2, chunks))
+        for m in pair:
+            strip_copy(m).wait()
+        if n == 0:
+            for i in range(2 * depth):
+                front_copy(i, i).start()
+        together(*[col_solve(m, strip.at[m - n]) for m in pair])
+    for copy in own_copies + piece_copies:
+        copy.wait()
+    together(row_solve(0, True, own_even, solved_even))
+
+    def two_blocks(pair, carry):
+        for odd in range(2):
+            step = 2 * pair + odd
+            slot = 2 * lax.rem(pair, depth) + odd
+            front_copy(step, slot).wait()
+
+            @pl.when(pair >= depth)
+            def _():
+                out_copy(step - 2 * depth, slot).wait()
+
+            if odd:
+                mine, later = (own_odd, solved_odd), (own_even, solved_even)
+            else:
+                mine, later = (own_even, solved_even), (own_odd, solved_odd)
+            together(update(step, slot, *mine), row_solve(jnp.minimum(step + 1, steps - 1), False, *later))
+            for q in range(fan):
+                outs[slot, :, q * local_rows : q * local_rows + held] = jnp.zeros((block_rows, held), F32)
+            if not odd:
+
+                @pl.when(pair == 0)
+                def _():
+                    outs[slot, :held, :] = jnp.zeros((held, local_cols), F32)
+
+            out_copy(step, slot).start()
+
+            @pl.when(pair + depth < steps // 2)
+            def _():
+                front_copy(step + 2 * depth, slot).start()
 
         return carry
 
-    lax.fori_loop(0, steps, work_rows, 0)
-    for i in range(max(0, steps - holds), steps):
-        out_copy(i, i % holds).wait()
+    lax.fori_loop(0, steps // 2, two_blocks, 0)
+    for i in range(steps - 2 * depth, steps):
+        out_copy(i, i % (2 * depth)).wait()
 
 
 def params():
@@ -488,6 +538,27 @@
     kid_of = (inverse_map >= row_map.shape[0] // 2).astype(F32)
     group_of = jnp.repeat(tile_group, MT // TS).astype(F32)
 
+    half_cost = pl.CostEstimate(flops=10**10, bytes_accessed=3 * 10**7, transcendentals=0)
+    work_shape = jax.ShapeDtypeStruct((PW, 2 * PW), F32)
+    begun, diag_col, diag_row, low_rows, piv_t, piv = pl.pallas_call(
+        functools.partial(open_kernel, (cols, fan, share, held, tiles)),
+        out_shape=[
+            work_shape,
+            jax.ShapeDtypeStruct((PW, 128), F32),
+            jax.ShapeDtypeStruct((8, PW), F32),
+            jax.ShapeDtypeStruct((PW, NPIV), F32),
+            jax.ShapeDtypeStruct((kid_cols, NPIV), BF16),
+            jax.ShapeDtypeStruct((NPIV, kid_cols), BF16),
+        ],
+        in_specs=[smem_spec()] * 3 + [whole_spec()] * 2,
+        out_specs=[whole_spec()] * 6,
+        scratch_shapes=[pltpu.VMEM((NPIV, NPIV), F32), pltpu.VMEM((NPIV, kid_cols), F32)],
+        compiler_params=params(),
+        cost_estimate=half_cost,
+        name="open_pivots",
+    )(place, group_of, kid_of, near, far)
+
+    begun, gathered = lax.optimization_barrier((begun, gathered))
     placed = pl.pallas_call(
         functools.partial(place_kernel, (cols, fan, tiles, slice_cols)),
         out_shape=[jax.ShapeDtypeStruct((2 * slice_cols, local_rows), BF16)] * cols,
@@ -497,29 +568,23 @@
         cost_estimate=pl.CostEstimate(flops=0, bytes_accessed=8 * 2**20, transcendentals=0),
         name="place_tiles",
     )(place, inverse_map, gathered)
-    near, far, *placed = lax.optimization_barrier((near, far, *placed))
+    begun, *placed = lax.optimization_barrier((begun, *placed))
     kid_parts = [swapped(placed[d], "col", d) for d in range(cols)]
     square = jax.ShapeDtypeStruct((PW, PW), BF16)
-    lower1, inv1_hi, inv1_lo, inv1_t_hi, inv1_t_lo, link, link_t, rest, piv_t, piv = pl.pallas_call(
-        functools.partial(first_kernel, (cols, fan, share, held, tiles)),
+    lower1, inv1_hi, inv1_lo, inv1_t_hi, inv1_t_lo, link, link_t, rest = pl.pallas_call(
+        first_kernel,
         out_shape=[
             jax.ShapeDtypeStruct((2 * PW, PW), F32),
             square, square, square, square, square, square,
             jax.ShapeDtypeStruct((PW, PW), F32),
-            jax.ShapeDtypeStruct((kid_cols, NPIV), BF16),
-            jax.ShapeDtypeStruct((NPIV, kid_cols), BF16),
         ],
-        in_specs=[smem_spec()] * 3 + [whole_spec()] * 2,
-        out_specs=[whole_spec()] * 10,
-        scratch_shapes=[
-            pltpu.VMEM((NPIV, NPIV), F32),
-            pltpu.VMEM((NPIV, kid_cols), F32),
-            pltpu.VMEM((PW, 2 * PW), F32),
-        ],
+        in_specs=[whole_spec()] * 4,
+        out_specs=[whole_spec()] * 8,
+        scratch_shapes=[pltpu.VMEM((PW, 2 * PW), F32)],
         compiler_params=params(),
-        cost_estimate=pl.CostEstimate(flops=2 * 10**10, bytes_accessed=5 * 10**7, transcendentals=0),
+        cost_estimate=half_cost,
         name="first_pivots",
-    )(place, group_of, kid_of, near, far)
+    )(begun, diag_col, diag_row, low_rows)
 
     rest, *arrived = lax.optimization_barrier((rest, *halves, *others))
     halves = [jnp.concatenate([arrived[h], arrived[2 + h]], axis=0) for h in range(2)]
@@ -534,7 +599,11 @@
         out_shape=[jax.ShapeDtypeStruct((PW, PW), F32), square, square, square, square],
         in_specs=[whole_spec()],
         out_specs=[whole_spec()] * 5,
-        scratch_shapes=[pltpu.VMEM((PW, 2 * PW), F32)],
+        scratch_shapes=[
+            pltpu.VMEM((PW, 2 * PW), F32),
+            pltpu.VMEM((PW, 128), F32),
+            pltpu.VMEM((8, PW), F32),
+        ],
         compiler_params=params(),
         cost_estimate=pl.CostEstimate(flops=2 * 10**10, bytes_accessed=5 * 10**7, transcendentals=0),
         name="second_pivots",
@@ -542,7 +611,7 @@
 
     block_rows = min(256, local_rows)
     wide = min(512, local_cols)
-    ins, holds = min(4, local_rows // block_rows), min(3, local_rows // block_rows)
+    depth = min(2, local_rows // block_rows // 2)
     schur_block, factor_panels = pl.pallas_call(
         functools.partial(
             schur_kernel,
@@ -556,17 +625,20 @@
         in_specs=[smem_spec()] * 3 + [whole_spec()] * 14 + [any_spec()] * (8 + cols),
         out_specs=[any_spec(), whole_spec()],
         scratch_shapes=[
-            pltpu.VMEM((ins, block_rows, local_cols), F32),
-            pltpu.VMEM((holds, block_rows, local_cols), F32),
+            pltpu.VMEM((2 * depth, block_rows, local_cols), F32),
+            pltpu.VMEM((2 * depth, block_rows, local_cols), F32),
             pltpu.VMEM((rows, held, local_cols), BF16),
             pltpu.VMEM((kid_cols, local_cols), BF16),
             pltpu.VMEM((kid_cols, local_rows), BF16),
             pltpu.VMEM((cols, local_rows, fan * held), F32),
             pltpu.VMEM((NPIV, local_cols), BF16),
-            pltpu.VMEM((NPIV, wide), F32),
+            pltpu.VMEM((2, NPIV, wide), F32),
             pltpu.VMEM((block_rows, NPIV), F32),
-            pltpu.SemaphoreType.DMA((ins,)),
-            pltpu.SemaphoreType.DMA((holds,)),
+            pltpu.VMEM((block_rows, NPIV), F32),
+            pltpu.VMEM((block_rows, kid_cols), BF16),
+            pltpu.VMEM((block_rows, kid_cols), BF16),
+            pltpu.SemaphoreType.DMA((2 * depth,)),
+            pltpu.SemaphoreType.DMA((2 * depth,)),
             pltpu.SemaphoreType.DMA((local_cols // wide,)),
             pltpu.SemaphoreType.DMA((fan,)),
             pltpu.SemaphoreType.DMA((cols,)),

time: 150 us -> 152 us (1.013)
  waiting for transfers between devices: 20.5 us -> 27.1 us
  Pallas kernels: 80.1 us -> 76.1 us
    ppermute x15, waiting for transfers between devices: 19.1 us -> 26.3 us  [swapped(): lax.ppermute(value, axis, [(i, i ^ mask) for i in range(lax.axis_size(axi...]
    pallas_call x1, Pallas kernels: 40.2 us -> 34.9 us  [local(): pl.pallas_call(functools.partial(schur_kernel, (rows, cols, fan, share, h...]
    pallas_call x1 -> x2, Pallas kernels: 19.4 us -> 20.9 us  [the longest x1 10.8 us: local(): pl.pallas_call(functools.partial(open_kernel, (cols, fan, share, held, ti...]
  transfers between devices with their start and end apart: 17 -> 17, of which waited for: 8 -> 7; matrix products, arithmetic and copies ran while one was open for 9% -> 9% of each run, Pallas kernels for 27% -> 27%
where the time goes in v2:
time: 152 us
  Pallas kernels  76.1 us (50%)
  waiting for transfers between devices  27.1 us (18%)
  starting transfers between devices  18.3 us (12%)
  between operations  14.3 us (9%)
  local copies, waits for them, and re-layouts  11.6 us (8%)
  other arithmetic  4.16 us (3%)
    pallas_call x1, Pallas kernels, local(): pl.pallas_call(functools.partial(schur_kernel, (rows, cols, fan, share, h...  34.9 us
    ppermute x15, waiting for transfers between devices, swapped(): lax.ppermute(value, axis, [(i, i ^ mask) for i in range(lax.axis_size(axi...  26.3 us
    ppermute x15, starting transfers between devices, swapped(): lax.ppermute(value, axis, [(i, i ^ mask) for i in range(lax.axis_size(axi...  18.2 us
    pallas_call x1, Pallas kernels, local(): pl.pallas_call(second_kernel, out_shape=[jax.ShapeDtypeStruct((PW, PW), F...  16.6 us
    pallas_call x1, Pallas kernels, local(): pl.pallas_call(functools.partial(open_kernel, (cols, fan, share, held, ti...  10.8 us
    pallas_call x1, Pallas kernels, local(): pl.pallas_call(first_kernel, out_shape=[jax.ShapeDtypeStruct((2 * PW, PW)...  10.1 us
    pallas_call x1, Pallas kernels, local(): pl.pallas_call(functools.partial(place_kernel, (cols, fan, tiles, slice_c...  3.68 us
  transfers between devices with their start and end apart: 17, of which 7 were waited for; matrix products, arithmetic and copies ran while one was open for 9% of the time, Pallas kernels for 27%

profile of v2, /device:TPU:0, one launch (start us, length us, event | category | flops | bytes accessed | tf_op | source)
XLA Modules:
  0.0 151.5 jit_solution(14205330122464501993)
XLA Ops:
  7.2 0.7 all-gather.5.cloned.1.call-update
  8.0 1.0 copy.6
  8.9 0.7 broadcast_compare_fusion
  10.1 0.9 fusion.2
  11.1 5.1 %collective-permute-start.2 = (f32[128,128]{1,0:T(8,128)S(1)}, f32[128,128]{1,0:T(8,128)S(1)}, u32[]{:S(2)}, u32[]{:S(2)}) collective-permute-start(f32[128,128]{1,0:T(8,128)S(1)} %maximum_maximum_fusion), channel_id=1, source_target_pairs={{0,24},{4,28},{8,16},{12,20},{16,8},{20,12},{24,0},{28,4},{1,25},{... | collective-permute-start | bytes 196616 | tf_op jit(solution)/shard_map/ppermute | solution.py:40
  16.9 2.1 %slice.170 = bf16[64,4096]{1,0:T(8,128)(2,1)} slice(f32[2048,4096]{1,0:T(8,128)} %refs_0_.1), slice={[0:64], [0:4096]} | slice | bytes 1048576 | tf_op jit(solution)/shard_map/slice | solution.py:519
  19.0 2.9 %collective-permute-done.1 = f32[128,128]{1,0:T(8,128)S(1)} collective-permute-done((f32[128,128]{1,0:T(8,128)S(1)}, f32[128,128]{1,0:T(8,128)S(1)}, u32[]{:S(2)}, u32[]{:S(2)}) %collective-permute-start.1) | collective-permute-done | bytes 65568 | tf_op jit(solution)/shard_map/ppermute | solution.py:40
  22.4 1.6 %collective-permute-start.4 = (f32[4,96,128]{2,1,0:T(8,128)S(1)}, f32[4,96,128]{2,1,0:T(8,128)S(1)}, u32[]{:S(2)}, u32[]{:S(2)}) collective-permute-start(f32[4,96,128]{2,1,0:T(8,128)S(1)} %get-tuple-element.117), channel_id=1, source_target_pairs={{0,2},{1,3},{2,0},{3,1},{4,6},{5,7},{6,4},{7,5},{8,10},{9,11},{10,... | collective-permute-start | bytes 589832 | tf_op jit(solution)/shard_map/ppermute | solution.py:40
  24.0 1.5 collective-permute-start.3
  25.9 2.9 %fusion.1 = (f32[2048,32]{1,0:T(8,128)S(1)}, f32[2048,32]{1,0:T(8,128)S(1)}, f32[2048,32]{1,0:T(8,128)S(1)}, f32[2048,32]{1,0:T(8,128)S(1)}) fusion(f32[2048,4096]{1,0:T(8,128)} %refs_0_.1), kind=kLoop, calls=%fused_computation.27 | loop fusion | bytes 2097152 | tf_op jit(solution)/shard_map/slice | solution.py:502
  29.3 2.5 %collective-permute-done.3 = f32[4,96,128]{2,1,0:T(8,128)S(1)} collective-permute-done((f32[4,96,128]{2,1,0:T(8,128)S(1)}, f32[4,96,128]{2,1,0:T(8,128)S(1)}, u32[]{:S(2)}, u32[]{:S(2)}) %collective-permute-start.3) | collective-permute-done | bytes 196640 | tf_op jit(solution)/shard_map/ppermute | solution.py:40
  31.8 2.6 %collective-permute-done.5 = f32[4,96,128]{2,1,0:T(8,128)S(1)} collective-permute-done((f32[4,96,128]{2,1,0:T(8,128)S(1)}, f32[4,96,128]{2,1,0:T(8,128)S(1)}, u32[]{:S(2)}, u32[]{:S(2)}) %collective-permute-start.5) | collective-permute-done | bytes 196640 | tf_op jit(solution)/shard_map/ppermute | solution.py:40
  34.5 0.9 pad_maximum_fusion
  35.5 1.7 %collective-permute-start.8 = (f32[1,1024,128]{2,1,0:T(8,128)S(1)}, f32[1,1024,128]{2,1,0:T(8,128)S(1)}, u32[]{:S(2)}, u32[]{:S(2)}) collective-permute-start(f32[1,1024,128]{2,1,0:T(8,128)S(1)} %get-tuple-element.74), channel_id=1, source_target_pairs={{0,2},{1,3},{2,0},{3,1},{4,6},{5,7},{6,4},{7,5},{8,10},{9,11},{10,... | collective-permute-start | bytes 1572872 | tf_op jit(solution)/shard_map/ppermute | solution.py:40
  37.2 1.5 collective-permute-start.7
  38.8 0.7 convert_element_type.19.group_of
  39.5 0.7 pad_add_fusion.place
  40.9 10.8 %open_pivots.1 = (f32[256,512]{1,0:T(8,128)}, f32[256,128]{1,0:T(8,128)}, f32[8,256]{1,0:T(8,128)}, f32[256,512]{1,0:T(8,128)}, bf16[256,512]{1,0:T(8,128)(2,1)}, /*index=5*/bf16[512,256]{1,0:T(8,128)(2,1)}) custom-call(s32[2]{0:T(128)} %pad_add_fusion.place, f32[128]{0:T(128)} %convert_element_type.19.group_of, f32[128]{0:T(128)} %compare_convert_fusion.kid_of, ...), custom_call_target="tpu_custom_call" | custom-call | flops 10000000000 | bytes 30000000 | tf_op jit(solution)/shard_map/open_pivots/pallas_call | solution.py:543
  51.7 3.7 %place_tiles.1 = (bf16[128,2048]{1,0:T(8,128)(2,1)}, bf16[128,2048]{1,0:T(8,128)(2,1)}, bf16[128,2048]{1,0:T(8,128)(2,1)}, bf16[128,2048]{1,0:T(8,128)(2,1)}) custom-call(s32[2]{0:T(128)} %pad_add_fusion.place, s32[128]{0:T(128)} %copy-done.9, bf16[8,64,2048]{2,1,0:T(8,128)(2,1)} %bitcast.24), custom_call_target="tpu_custom_call" | custom-call | bytes 8388608 | tf_op jit(solution)/shard_map/place_tiles/pallas_call | solution.py:562
  55.4 0.8 collective-permute-start.9
  56.4 2.5 %collective-permute-start.11 = (bf16[128,2048]{1,0:T(8,128)(2,1)}, bf16[128,2048]{1,0:T(8,128)(2,1)}, u32[]{:S(2)}, u32[]{:S(2)}) collective-permute-start(bf16[128,2048]{1,0:T(8,128)(2,1)} %get-tuple-element.80), channel_id=1, source_target_pairs={{0,3},{1,2},{2,1},{3,0},{4,7},{5,6},{6,5},{7,4},{8,11},{9,10},{10,... | collective-permute-start | bytes 1572872 | tf_op jit(solution)/shard_map/ppermute | solution.py:40
  58.9 10.1 %first_pivots.1 = (f32[512,256]{1,0:T(8,128)}, bf16[256,256]{1,0:T(8,128)(2,1)}, bf16[256,256]{1,0:T(8,128)(2,1)}, bf16[256,256]{1,0:T(8,128)(2,1)}, bf16[256,25...) custom-call(f32[256,512]{1,0:T(8,128)} %get-tuple-element.66.begun, ...), custom_call_target="tpu_custom_call" | custom-call | flops 10000000000 | bytes 30000000 | tf_op jit(solution)/shard_map/first_pivots/pallas_call | solution.py:574
  69.0 0.8 copy-done.4
  69.9 1.0 copy-done.5
  71.0 10.3 %collective-permute-done.10.refs_6_ = bf16[128,2048]{1,0:T(8,128)(2,1)} collective-permute-done((bf16[128,2048]{1,0:T(8,128)(2,1)}, bf16[128,2048]{1,0:T(8,128)(2,1)}, u32[]{:S(2)}, u32[]{:S(2)}) %collective-permute-start.10) | collective-permute-done | bytes 524320 | tf_op jit(solution)/shard_map/ppermute | solution.py:40
  81.4 1.0 slice.143
  82.4 1.0 slice.144
  83.5 0.9 collective-permute-start.13
  84.5 1.1 collective-permute-start.14
  85.6 16.6 %second_pivots.1 = (f32[256,256]{1,0:T(8,128)}, bf16[256,256]{1,0:T(8,128)(2,1)}, bf16[256,256]{1,0:T(8,128)(2,1)}, bf16[256,256]{1,0:T(8,128)(2,1)}, bf16[256,256]{1,0:T(8,128)(2,1)}) custom-call(f32[256,256]{1,0:T(8,128)} %get-tuple-element.86.rest), custom_call_target="tpu_custom_call" | custom-call | flops 20000000000 | bytes 50000000 | tf_op jit(solution)/shard_map/second_pivots/pallas_call | solution.py:597
  102.2 7.0 %collective-permute-done.13.refs_9_ = f32[2,1024,128]{2,1,0:T(8,128)} collective-permute-done((f32[2,1024,128]{2,1,0:T(8,128)S(1)}, f32[2,1024,128]{2,1,0:T(8,128)}, u32[]{:S(2)}, u32[]{:S(2)}) %collective-permute-start.13) | collective-permute-done | bytes 1048608 | tf_op jit(solution)/shard_map/ppermute | solution.py:40
  109.8 34.9 %schur_update.1 = (f32[2048,4096]{1,0:T(8,128)}, bf16[2048,128]{1,0:T(8,128)(2,1)}) custom-call(s32[2]{0:T(128)} %pad_add_fusion.place, f32[128]{0:T(128)} %convert_element_type.19.group_of, f32[128]{0:T(128)} %compare_convert_fusion.kid_of, bf16[512,256]{1,0:T(8,128)(2,1)} %get-tuple-element.57.piv, bf16[256,512]{1,0:T(8,128)(2,1)} %get-tuple-element.58.piv_t, ...), custom_call_target="tpu_custom_call" | custom-call | flops 30000001024 | bytes 90000000 | tf_op jit(solution)/shard_map/schur_update/pallas_call | solution.py:615
  (68 shorter events, 4.8 us)
Async XLA Ops:
  7.2 44.5 %all-gather.5.cloned.1.call-start = ((), (), s32[]{:S(2)}) async-start(), calls=%async_computation | async-start | bytes 2359296 | tf_op jit(solution)/shard_map/all_gather | solution.py:518
  7.9 101.9 %all-gather.7.cloned.1.call-start = ((), (), s32[]{:S(2)}) async-start(), calls=%async_computation.1 | async-start | bytes 4718592 | tf_op jit(solution)/shard_map/all_gather | solution.py:520
  11.1 7.8 %collective-permute-start.2 = (f32[128,128]{1,0:T(8,128)S(1)}, f32[128,128]{1,0:T(8,128)S(1)}, u32[]{:S(2)}, u32[]{:S(2)}) collective-permute-start(f32[128,128]{1,0:T(8,128)S(1)} %maximum_maximum_fusion), channel_id=1, source_target_pairs={{0,24},{4,28},{8,16},{12,20},{16,8},{20,12},{24,0},{28,4},{1,25},{... | collective-permute-start | bytes 196616 | tf_op jit(solution)/shard_map/ppermute | solution.py:40
  16.2 5.6 %collective-permute-start.1 = (f32[128,128]{1,0:T(8,128)S(1)}, f32[128,128]{1,0:T(8,128)S(1)}, u32[]{:S(2)}, u32[]{:S(2)}) collective-permute-start(f32[128,128]{1,0:T(8,128)S(1)} %maximum_maximum_fusion), channel_id=1, source_target_pairs={{0,16},{4,20},{8,24},{12,28},{16,0},{20,4},{24,8},{28,12},{1,17},{... | collective-permute-start | bytes 196616 | tf_op jit(solution)/shard_map/ppermute | solution.py:40
  16.2 5.6 %collective-permute-start = (f32[128,128]{1,0:T(8,128)S(1)}, f32[128,128]{1,0:T(8,128)S(1)}, u32[]{:S(2)}, u32[]{:S(2)}) collective-permute-start(f32[128,128]{1,0:T(8,128)S(1)} %maximum_maximum_fusion), channel_id=1, source_target_pairs={{0,8},{4,12},{8,0},{12,4},{16,24},{20,28},{24,16},{28,20},{1,9},{5... | collective-permute-start | bytes 196616 | tf_op jit(solution)/shard_map/ppermute | solution.py:40
  22.4 6.9 %collective-permute-start.4 = (f32[4,96,128]{2,1,0:T(8,128)S(1)}, f32[4,96,128]{2,1,0:T(8,128)S(1)}, u32[]{:S(2)}, u32[]{:S(2)}) collective-permute-start(f32[4,96,128]{2,1,0:T(8,128)S(1)} %get-tuple-element.117), channel_id=1, source_target_pairs={{0,2},{1,3},{2,0},{3,1},{4,6},{5,7},{6,4},{7,5},{8,10},{9,11},{10,... | collective-permute-start | bytes 589832 | tf_op jit(solution)/shard_map/ppermute | solution.py:40
  24.0 7.8 %collective-permute-start.3 = (f32[4,96,128]{2,1,0:T(8,128)S(1)}, f32[4,96,128]{2,1,0:T(8,128)S(1)}, u32[]{:S(2)}, u32[]{:S(2)}) collective-permute-start(f32[4,96,128]{2,1,0:T(8,128)S(1)} %get-tuple-element.117), channel_id=1, source_target_pairs={{0,1},{1,0},{2,3},{3,2},{4,5},{5,4},{6,7},{7,6},{8,9},{9,8},{10,11... | collective-permute-start | bytes 589832 | tf_op jit(solution)/shard_map/ppermute | solution.py:40
  25.5 8.9 %collective-permute-start.5 = (f32[4,96,128]{2,1,0:T(8,128)S(1)}, f32[4,96,128]{2,1,0:T(8,128)S(1)}, u32[]{:S(2)}, u32[]{:S(2)}) collective-permute-start(f32[4,96,128]{2,1,0:T(8,128)S(1)} %get-tuple-element.117), channel_id=1, source_target_pairs={{0,3},{1,2},{2,1},{3,0},{4,7},{5,6},{6,5},{7,4},{8,11},{9,10},{10,... | collective-permute-start | bytes 589832 | tf_op jit(solution)/shard_map/ppermute | solution.py:40
  34.4 1.0 copy-start.3
  34.4 6.4 %collective-permute-start.6 = (f32[4,4,96,128]{3,2,1,0:T(8,128)S(1)}, f32[4,4,96,128]{3,2,1,0:T(8,128)}, u32[]{:S(2)}, u32[]{:S(2)}) collective-permute-start(f32[4,4,96,128]{3,2,1,0:T(8,128)S(1)} %pad_maximum_fusion.4.near), channel_id=1, source_target_pairs={{0,4},{4,0},{8,12},{12,8},{16,20},{20,16},{24,28},{28,24},{1,5},{5... | collective-permute-start | bytes 2359304 | tf_op jit(solution)/shard_map/ppermute | solution.py:40
  35.4 3.3 %copy-start.10 = (s32[32]{0:T(128)S(1)}, s32[32]{0:T(128)}, u32[]{:S(2)}) copy-start(s32[32]{0:T(128)} %param.5) | copy-start | bytes 388
  35.4 4.7 %copy-start.8 = (s32[128]{0:T(128)S(1)}, s32[128]{0:T(128)}, u32[]{:S(2)}) copy-start(s32[128]{0:T(128)} %param.7) | copy-start | bytes 1540
  35.5 33.5 %collective-permute-start.8 = (f32[1,1024,128]{2,1,0:T(8,128)S(1)}, f32[1,1024,128]{2,1,0:T(8,128)S(1)}, u32[]{:S(2)}, u32[]{:S(2)}) collective-permute-start(f32[1,1024,128]{2,1,0:T(8,128)S(1)} %get-tuple-element.74), channel_id=1, source_target_pairs={{0,2},{1,3},{2,0},{3,1},{4,6},{5,7},{6,4},{7,5},{8,10},{9,11},{10,... | collective-permute-start | bytes 1572872 | tf_op jit(solution)/shard_map/ppermute | solution.py:40
  37.2 31.8 %collective-permute-start.7 = (f32[1,1024,128]{2,1,0:T(8,128)S(1)}, f32[1,1024,128]{2,1,0:T(8,128)S(1)}, u32[]{:S(2)}, u32[]{:S(2)}) collective-permute-start(f32[1,1024,128]{2,1,0:T(8,128)S(1)} %get-tuple-element.72), channel_id=1, source_target_pairs={{0,1},{1,0},{2,3},{3,2},{4,5},{5,4},{6,7},{7,6},{8,9},{9,8},{10,11... | collective-permute-start | bytes 1572872 | tf_op jit(solution)/shard_map/ppermute | solution.py:40
  40.3 11.4 %copy-start.9 = (s32[128]{0:T(128)}, s32[128]{0:T(128)S(1)}, u32[]{:S(2)}) copy-start(s32[128]{0:T(128)S(1)} %select_reduce_fusion.inverse_map) | copy-start | bytes 1540
  55.4 15.5 %collective-permute-start.9 = (bf16[128,2048]{1,0:T(8,128)(2,1)}, bf16[128,2048]{1,0:T(8,128)(2,1)S(1)}, u32[]{:S(2)}, u32[]{:S(2)}) collective-permute-start(bf16[128,2048]{1,0:T(8,128)(2,1)} %get-tuple-element.78), channel_id=1, source_target_pairs={{0,1},{1,0},{2,3},{3,2},{4,5},{5,4},{6,7},{7,6},{8,9},{9,8},{10,11... | collective-permute-start | bytes 1572872 | tf_op jit(solution)/shard_map/ppermute | solution.py:40
  56.2 25.1 %collective-permute-start.10 = (bf16[128,2048]{1,0:T(8,128)(2,1)}, bf16[128,2048]{1,0:T(8,128)(2,1)}, u32[]{:S(2)}, u32[]{:S(2)}) collective-permute-start(bf16[128,2048]{1,0:T(8,128)(2,1)} %get-tuple-element.79), channel_id=1, source_target_pairs={{0,2},{1,3},{2,0},{3,1},{4,6},{5,7},{6,4},{7,5},{8,10},{9,11},{10,... | collective-permute-start | bytes 1572872 | tf_op jit(solution)/shard_map/ppermute | solution.py:40
  56.4 24.9 %collective-permute-start.11 = (bf16[128,2048]{1,0:T(8,128)(2,1)}, bf16[128,2048]{1,0:T(8,128)(2,1)}, u32[]{:S(2)}, u32[]{:S(2)}) collective-permute-start(bf16[128,2048]{1,0:T(8,128)(2,1)} %get-tuple-element.80), channel_id=1, source_target_pairs={{0,3},{1,2},{2,1},{3,0},{4,7},{5,6},{6,5},{7,4},{8,11},{9,10},{10,... | collective-permute-start | bytes 1572872 | tf_op jit(solution)/shard_map/ppermute | solution.py:40
  69.0 0.8 copy-start.4
  69.8 1.0 copy-start.5
  69.8 11.5 %copy-start.6 = (bf16[128,2048]{1,0:T(8,128)(2,1)S(1)}, bf16[128,2048]{1,0:T(8,128)(2,1)}, u32[]{:S(2)}) copy-start(bf16[128,2048]{1,0:T(8,128)(2,1)} %get-tuple-element.82.refs_4_) | copy-start | bytes 1572868
  70.9 12.6 %copy-start = (f32[2,1024,128]{2,1,0:T(8,128)}, f32[2,1024,128]{2,1,0:T(8,128)S(1)}, u32[]{:S(2)}) copy-start(f32[2,1024,128]{2,1,0:T(8,128)S(1)} %pad_maximum_fusion.1.refs_8_) | copy-start | bytes 3145732
  70.9 13.5 %copy-start.1 = (f32[2,1024,128]{2,1,0:T(8,128)}, f32[2,1024,128]{2,1,0:T(8,128)S(1)}, u32[]{:S(2)}) copy-start(f32[2,1024,128]{2,1,0:T(8,128)S(1)} %pad_maximum_fusion.2.refs_10_) | copy-start | bytes 3145732
  71.0 11.4 %copy-start.7 = (bf16[128,2048]{1,0:T(8,128)(2,1)}, bf16[128,2048]{1,0:T(8,128)(2,1)S(1)}, u32[]{:S(2)}) copy-start(bf16[128,2048]{1,0:T(8,128)(2,1)S(1)} %collective-permute-done.9.refs_5_) | copy-start | bytes 1572868
  83.4 18.7 %copy-start.2 = (bf16[256,2048]{1,0:T(8,128)(2,1)}, bf16[256,2048]{1,0:T(8,128)(2,1)S(1)}, u32[]{:S(2)}) copy-start(bf16[256,2048]{1,0:T(8,128)(2,1)S(1)} %pad_maximum_fusion.3.refs_2_) | copy-start | bytes 3145732
  83.4 18.7 %collective-permute-start.12 = (bf16[256,2048]{1,0:T(8,128)(2,1)S(1)}, bf16[256,2048]{1,0:T(8,128)(2,1)}, u32[]{:S(2)}, u32[]{:S(2)}) collective-permute-start(bf16[256,2048]{1,0:T(8,128)(2,1)S(1)} %pad_maximum_fusion.3.refs_2_), channel_id=1, source_target_pairs={{0,4},{4,0},{8,12},{12,8},{16,20},{20,16},{24,28},{28,24},{1,5},{5... | collective-permute-start | bytes 3145736 | tf_op jit(solution)/shard_map/ppermute | solution.py:40
  83.5 25.7 %collective-permute-start.13 = (f32[2,1024,128]{2,1,0:T(8,128)S(1)}, f32[2,1024,128]{2,1,0:T(8,128)}, u32[]{:S(2)}, u32[]{:S(2)}) collective-permute-start(f32[2,1024,128]{2,1,0:T(8,128)S(1)} %pad_maximum_fusion.1.refs_8_), channel_id=1, source_target_pairs={{0,2},{1,3},{2,0},{3,1},{4,6},{5,7},{6,4},{7,5},{8,10},{9,11},{10,... | collective-permute-start | bytes 3145736 | tf_op jit(solution)/shard_map/ppermute | solution.py:40
  84.5 25.3 %collective-permute-start.14 = (f32[2,1024,128]{2,1,0:T(8,128)S(1)}, f32[2,1024,128]{2,1,0:T(8,128)}, u32[]{:S(2)}, u32[]{:S(2)}) collective-permute-start(f32[2,1024,128]{2,1,0:T(8,128)S(1)} %pad_maximum_fusion.2.refs_10_), channel_id=1, source_target_pairs={{0,1},{1,0},{2,3},{3,2},{4,5},{5,4},{6,7},{7,6},{8,9},{9,8},{10,11... | collective-permute-start | bytes 3145736 | tf_op jit(solution)/shard_map/ppermute | solution.py:40
Sparse Core Ops, SparseCore 0:
  9.6 31.7 all-gather.4
  43.0 46.7 all-gather.6

commit v3 on v2

--- a/solution.py
+++ b/solution.py
@@ -19,6 +19,7 @@
 
 NN = (((1,), (0,)), ((), ()))
 NT = (((1,), (1,)), ((), ()))
+TN = (((0,), (0,)), ((), ()))
 
 
 def dot(left, right, dims=NN, precision=None):
@@ -97,27 +98,32 @@
     return jnp.concatenate([work[g] * scale[g] for g in range(groups)], axis=0)
 
 
-def factor_panel(work, start, stop):
+def factor_panel(work, upper_out):
     per_tile = 128 // BLK
-    row = lax.broadcasted_iota(jnp.int32, (PW, BLK), 0)
-    lane = lax.broadcasted_iota(jnp.int32, (BLK, 128), 1)
+    row = lax.broadcasted_iota(jnp.int32, (BLK, PW), 0)
+    lane = lax.broadcasted_iota(jnp.int32, (BLK, PW), 1)
+    all_lane = lax.broadcasted_iota(jnp.int32, (PW, PW), 1)
 
     def step(b, carry):
         low = pl.multiple_of(b * BLK, BLK)
         tile = pl.multiple_of((b // per_tile) * 128, 128)
-        turn = (128 - (b % per_tile) * BLK) % 128
-        columns = pltpu.roll(work[:, pl.ds(tile, 128)], turn, 1)
-        block = pltpu.roll(work[pl.ds(low, BLK), pl.ds(tile, 128)], turn, 1)
+        shift = (b % per_tile) * BLK
+        block = pltpu.roll(work[pl.ds(low, BLK), pl.ds(tile, 128)], (128 - shift) % 128, 1)
         done = factor_diagonal(block)
-        inverse = jnp.where(lane < BLK, pltpu.roll(done, 128 - BLK, 1), 0.0)
-        upper = exact(inverse[:, :BLK], work[pl.ds(low, BLK), :])
-        lead = exact(columns, inverse, NT)
-        lead = jnp.where(row >= low + BLK, lead, 0.0)
-        work[...] = work[...] - exact(lead, upper)
+        inverse = pltpu.roll(done, 128 - BLK, 1)[:, :BLK]
+        inside = (lane >= low) & (lane < low + BLK)
+        lines = jnp.where(inside, jnp.where(lane == row + low, 1.0, 0.0), work[pl.ds(low, BLK), :])
+        upper = exact(inverse, lines)
+        placed = pltpu.roll(done, shift, 1)
+        corner = jnp.concatenate([placed] * (PW // 128), axis=1)
+        upper_out[pl.ds(low, BLK), :] = jnp.where(inside, corner, upper)
+        lead = jnp.where(lane >= low + BLK, upper, 0.0)
+        kept = jnp.where((all_lane >= low) & (all_lane < low + BLK), 0.0, work[...])
+        work[...] = kept - exact(lead, upper, TN)
         work[pl.ds(low, BLK), :] = upper
         return carry
 
-    lax.fori_loop(start, stop, step, 0)
+    lax.fori_loop(0, PW // BLK, step, 0)
 
 
 def diagonals(value):
@@ -131,8 +137,7 @@
     by_row, by_col = diagonals(value)
     diag_col[...] = jnp.broadcast_to(by_row, (PW, 128))
     diag_row[...] = jnp.broadcast_to(by_col, (8, PW))
-    work[:, :PW] = value / jnp.sqrt(by_row) / jnp.sqrt(by_col)
-    work[:, PW:] = unit()
+    work[...] = value / jnp.sqrt(by_row) / jnp.sqrt(by_col)
 
 
 def pivot_values(table, stride, share, along_rows):
@@ -148,24 +153,19 @@
     return jnp.concatenate([jnp.full((1, TS), table[start + i], F32) for i in range(count)], axis=1)
 
 
-def finish_panel(work, diag_col, diag_row, lower, inv_hi, inv_lo, inv_t_hi, inv_t_lo):
+def finish_panel(work, upper, diag_col, diag_row, lower, inv_hi, inv_lo, inv_t_hi, inv_t_lo):
     row = lax.broadcasted_iota(jnp.int32, (PW, PW), 0)
     col = lax.broadcasted_iota(jnp.int32, (PW, PW), 1)
-    lower[:PW, :] = jnp.where(col <= row, work[:, :PW].T, 0.0) * jnp.sqrt(diag_col[:, :1])
-    inverse = work[:, PW:] / jnp.sqrt(diag_row[:1, :])
+    lower[:PW, :] = jnp.where(col <= row, upper[...].T, 0.0) * jnp.sqrt(diag_col[:, :1])
+    inverse = jnp.where(col <= row, work[...], 0.0) / jnp.sqrt(diag_row[:1, :])
     inv_hi[...], inv_lo[...] = split(inverse)
     inv_t_hi[...], inv_t_lo[...] = split(inverse.T)
     return inverse
 
 
-def unit():
-    row = lax.broadcasted_iota(jnp.int32, (PW, PW), 0)
-    col = lax.broadcasted_iota(jnp.int32, (PW, PW), 1)
-    return jnp.where(row == col, 1.0, 0.0)
-
-
-def open_kernel(sizes, place, group_of, kid_of, near, far,
-                work, diag_col, diag_row, low_rows, piv_t, piv, pile, wide):
+def first_kernel(sizes, place, group_of, kid_of, near, far,
+                 lower, inv_hi, inv_lo, inv_t_hi, inv_t_lo, link_out, link_t, rest, piv_t, piv,
+                 pile, wide, work, upper, diag_col, diag_row):
     cols, fan, share, held, tiles = sizes
     my_row, my_col = place[0], place[1]
     my_q, my_a = my_row % fan, my_row // fan
@@ -193,27 +193,20 @@
     same_group = pivot_values(group_of, tiles, share, True) == pivot_values(group_of, tiles, share, False)
     same_kid = pivot_values(kid_of, tiles, share, True) == pivot_values(kid_of, tiles, share, False)
     pile[...] = jnp.where(same_group, pile[...], 0.0) + jnp.where(same_kid, product, 0.0)
-    low_rows[...] = pile[PW:, :]
     start_panel(work, diag_col, diag_row, pile[:PW, :PW])
-    factor_panel(work, 0, PW // BLK // 2)
-
-
-def first_kernel(begun, diag_col, diag_row, low_rows,
-                 lower, inv_hi, inv_lo, inv_t_hi, inv_t_lo, link_out, link_t, rest, work):
-    work[...] = begun[...]
-    factor_panel(work, PW // BLK // 2, PW // BLK)
-    inverse = finish_panel(work, diag_col, diag_row, lower, inv_hi, inv_lo, inv_t_hi, inv_t_lo)
-    link = exact(low_rows[:, :PW], inverse, NT).astype(BF16)
+    factor_panel(work, upper)
+    inverse = finish_panel(work, upper, diag_col, diag_row, lower, inv_hi, inv_lo, inv_t_hi, inv_t_lo)
+    link = exact(pile[PW:, :PW], inverse, NT).astype(BF16)
     link_out[...] = link
     lower[PW:, :] = link.astype(F32)
     link_t[...] = link.astype(F32).T.astype(BF16)
-    rest[...] = low_rows[:, PW:] - dot(link, link, NT)
-
-
-def second_kernel(rest, lower, inv_hi, inv_lo, inv_t_hi, inv_t_lo, work, diag_col, diag_row):
+    rest[...] = pile[PW:, PW:] - dot(link, link, NT)
+
+
+def second_kernel(rest, lower, inv_hi, inv_lo, inv_t_hi, inv_t_lo, work, upper, diag_col, diag_row):
     start_panel(work, diag_col, diag_row, rest[...])
-    factor_panel(work, 0, PW // BLK)
-    finish_panel(work, diag_col, diag_row, lower, inv_hi, inv_lo, inv_t_hi, inv_t_lo)
+    factor_panel(work, upper)
+    finish_panel(work, upper, diag_col, diag_row, lower, inv_hi, inv_lo, inv_t_hi, inv_t_lo)
 
 
 def place_kernel(sizes, place, inverse_map, held, *outs):
@@ -235,23 +228,80 @@
             outs[d][slice_cols:, i * TS : (i + 1) * TS] = fetch((my_col ^ d) * fan + my_q, i)
 
 
+def together(*parts):
+    parts = list(parts)
+    while parts:
+        for part in list(parts):
+            try:
+                next(part)
+            except StopIteration:
+                parts.remove(part)
+
+
+def col_kernel(sizes, place, group_of, kid_of, strips, near_kids, far_kids,
+               piv, inv1_hi, inv1_lo, inv2_hi, inv2_lo, link, out, strip, kids):
+    rows, fan, share, block_cols, local_rows, tiles, wide = sizes
+    my_row, my_col = place[0], place[1]
+    my_q = my_row % fan
+    j = pl.program_id(0)
+    q = (j * block_cols) // local_rows
+    group_col = pivot_values(group_of, tiles, share, True)
+    kid_col = pivot_values(kid_of, tiles, share, True)
+
+    @pl.when(q == my_q)
+    def _():
+        kids[...] = near_kids[...]
+
+    @pl.when(q != my_q)
+    def _():
+        kids[...] = far_kids[...]
+
+    def col_solve(n, pile):
+        at = slice(n * wide, (n + 1) * wide)
+        for r in range(rows):
+            piece = strips[r, :, at].astype(F32)
+            for k in range(NP):
+                low = k * PW + r * share
+                pile[low : low + share, :] = piece[k * share : (k + 1) * share]
+        tile = my_col * fan * tiles + (j * block_cols + n * wide) // TS
+        group_all = tile_values(group_of, tile, wide // TS)
+        kid_all = tile_values(kid_of, tile, wide // TS)
+        product = dot(piv[...], kids[:, at])
+        yield
+        full = jnp.where(group_col == group_all, pile[...], 0.0) + jnp.where(
+            kid_col == kid_all, product, 0.0
+        )
+        first, second = full[:PW].astype(BF16), full[PW:]
+        yield
+        both = dot(jnp.concatenate([inv1_hi[...], inv1_lo[...]], axis=0), first)
+        yield
+        head = (both[:PW] + both[PW:]).astype(BF16)
+        out[:PW, at] = -head
+        yield
+        second = (second - dot(link[...], head)).astype(BF16)
+        yield
+        both = dot(jnp.concatenate([inv2_hi[...], inv2_lo[...]], axis=0), second)
+        yield
+        out[PW:, at] = (-(both[:PW] + both[PW:])).astype(BF16)
+
+    together(*[col_solve(n, strip.at[n]) for n in range(block_cols // wide)])
+
+
 def schur_kernel(sizes, masks, place, group_of, kid_of,
-                 piv, piv_t, lower1, lower2, inv1_hi, inv1_lo, inv2_hi, inv2_lo, link,
-                 inv1_t_hi, inv1_t_lo, inv2_t_hi, inv2_t_lo, link_t, *refs):
-    rows, cols, fan, share, held, slice_cols, block_rows, local_rows, local_cols, tiles, wide = sizes
-    front, strips, near_kids, far_kids = refs[:4]
+                 piv_t, lower1, lower2, inv1_t_hi, inv1_t_lo, inv2_t_hi, inv2_t_lo, link_t, *refs):
+    cols, fan, share, held, slice_cols, block_rows, local_rows, local_cols, tiles = sizes
+    front, solved_cols, near_kids, far_kids = refs[:4]
     sources = refs[4 : 4 + cols]
-    halves = [refs[4 + cols : 6 + cols], refs[6 + cols : 8 + cols]]
-    out, panel = refs[8 + cols : 10 + cols]
-    (fronts, outs, strips_in, kids, own_t, pieces, flipped, strip, solved_even, solved_odd, own_even, own_odd,
-     front_sems, out_sems, strip_sems, kid_sems, own_sems, piece_sems) = refs[10 + cols :]
+    quarters = refs[4 + cols : 12 + cols]
+    out, panel = refs[12 + cols : 14 + cols]
+    (fronts, outs, kids, own_t, pieces, flipped, solved_even, solved_odd, own_even, own_odd,
+     front_sems, out_sems, flip_sem, kid_sems, own_sems, piece_sems) = refs[14 + cols :]
     my_row, my_col = place[0], place[1]
     my_q = my_row % fan
     first_tile = my_col * fan * tiles
     steps = local_rows // block_rows
-    chunks = local_cols // wide
     depth = fronts.shape[0] // 2
-    half_rows = local_rows // 2
+    quarter_rows = local_rows // 4
 
     def rows_at(i):
         return pl.ds(pl.multiple_of(i * block_rows, block_rows), block_rows)
@@ -261,14 +311,6 @@
 
     def out_copy(i, slot):
         return pltpu.make_async_copy(outs.at[slot], out.at[rows_at(i), :], out_sems.at[slot])
-
-    def chunk_at(n):
-        return pl.ds(pl.multiple_of(n * wide, wide), wide)
-
-    def strip_copy(n):
-        return pltpu.make_async_copy(
-            strips.at[:, :, chunk_at(n)], strips_in.at[:, :, chunk_at(n)], strip_sems.at[n]
-        )
 
     kid_copies = [
         pltpu.make_async_copy(
@@ -278,6 +320,7 @@
         )
         for q, source in enumerate((near_kids, far_kids))
     ]
+    flip_copy = pltpu.make_async_copy(solved_cols, flipped, flip_sem)
     own_copies = [
         pltpu.make_async_copy(
             source.at[:slice_cols, :], own_t.at[d * slice_cols : (d + 1) * slice_cols, :], own_sems.at[d]
@@ -286,52 +329,19 @@
     ]
     piece_copies = [
         pltpu.make_async_copy(
-            halves[half][i // (cols // 2)].at[i % (cols // 2)],
-            pieces.at[my_col ^ mask, half * half_rows : (half + 1) * half_rows, :],
-            piece_sems.at[half * cols + i],
+            quarters[2 * quarter + i // (cols // 2)].at[i % (cols // 2)],
+            pieces.at[my_col ^ mask, quarter * quarter_rows : (quarter + 1) * quarter_rows, :],
+            piece_sems.at[quarter * cols + i],
         )
-        for half in range(2)
-        for i, mask in enumerate(masks[half])
+        for quarter in range(4)
+        for i, mask in enumerate(masks[quarter // 2])
     ]
-    for copy in kid_copies:
+    for copy in own_copies + piece_copies + [flip_copy] + kid_copies:
         copy.start()
-    for n in range(chunks):
-        strip_copy(n).start()
+    for i in range(2 * depth):
+        front_copy(i, i).start()
     for copy in own_copies + piece_copies:
-        copy.start()
-    for copy in kid_copies:
         copy.wait()
-    group_col = pivot_values(group_of, tiles, share, True)
-    kid_col = pivot_values(kid_of, tiles, share, True)
-
-    def col_solve(n, pile):
-        at = slice(n * wide, (n + 1) * wide)
-        for r in range(rows):
-            piece = strips_in[r, :, at].astype(F32)
-            for k in range(NP):
-                low = k * PW + r * share
-                pile[low : low + share, :] = piece[k * share : (k + 1) * share]
-        tile = first_tile + n * (wide // TS)
-        group_all = tile_values(group_of, tile, wide // TS)
-        kid_all = tile_values(kid_of, tile, wide // TS)
-        product = dot(piv[...], kids[:, at])
-        yield
-        full = jnp.where(group_col == group_all, pile[...], 0.0) + jnp.where(
-            kid_col == kid_all, product, 0.0
-        )
-        first, second = full[:PW].astype(BF16), full[PW:]
-        yield
-        both = dot(jnp.concatenate([inv1_hi[...], inv1_lo[...]], axis=0), first)
-        yield
-        head = (both[:PW] + both[PW:]).astype(BF16)
-        flipped[:PW, at] = -head
-        yield
-        second = (second - dot(link[...], head)).astype(BF16)
-        yield
-        both = dot(jnp.concatenate([inv2_hi[...], inv2_lo[...]], axis=0), second)
-        yield
-        flipped[PW:, at] = (-(both[:PW] + both[PW:])).astype(BF16)
-
     col_share = PW // cols
     subs = block_rows // TS
     per_tile = 128 // col_share
@@ -403,26 +413,9 @@
                 )
             yield
 
-    def together(*parts):
-        parts = list(parts)
-        while parts:
-            for part in list(parts):
-                try:
-                    next(part)
-                except StopIteration:
-                    parts.remove(part)
-
-    for n in range(0, chunks, 2):
-        pair = range(n, min(n + 2, chunks))
-        for m in pair:
-            strip_copy(m).wait()
-        if n == 0:
-            for i in range(2 * depth):
-                front_copy(i, i).start()
-        together(*[col_solve(m, strip.at[m - n]) for m in pair])
-    for copy in own_copies + piece_copies:
+    together(row_solve(0, True, own_even, solved_even))
+    for copy in [flip_copy] + kid_copies:
         copy.wait()
-    together(row_solve(0, True, own_even, solved_even))
 
     def two_blocks(pair, carry):
         for odd in range(2):
@@ -505,6 +498,11 @@
         ],
         axis=1,
     )
+    gathered = lax.all_gather(flipped, "row", axis=0)
+    col_strip, row_strip, *packets = lax.optimization_barrier(
+        (front_entries[:held].astype(BF16), row_strip, *packets)
+    )
+    col_strips = lax.all_gather(col_strip, "row", axis=0)
     steps = [1 << i for i in range(cols.bit_length() - 1)]
     orders = [steps, steps[::-1]]
     halves = [row_strip[None, : local_rows // 2], row_strip[None, local_rows // 2 :]]
@@ -515,9 +513,6 @@
             masks[h] = masks[h] + [m ^ step for m in masks[h]]
     others = [swapped(halves[h], "col", orders[h][-2]) for h in range(2)]
     masks = [masks[h] + [m ^ orders[h][-2] for m in masks[h]] for h in range(2)]
-    gathered = lax.all_gather(flipped, "row", axis=0)
-    col_strip, *packets = lax.optimization_barrier((front_entries[:held].astype(BF16), *packets))
-    col_strips = lax.all_gather(col_strip, "row", axis=0)
     merged = []
     for d in range(cols):
         kid = packets[d][held:, :held] + packets[d ^ (cols // 2)][held:, held:]
@@ -538,121 +533,143 @@
     kid_of = (inverse_map >= row_map.shape[0] // 2).astype(F32)
     group_of = jnp.repeat(tile_group, MT // TS).astype(F32)
 
-    half_cost = pl.CostEstimate(flops=10**10, bytes_accessed=3 * 10**7, transcendentals=0)
-    work_shape = jax.ShapeDtypeStruct((PW, 2 * PW), F32)
-    begun, diag_col, diag_row, low_rows, piv_t, piv = pl.pallas_call(
-        functools.partial(open_kernel, (cols, fan, share, held, tiles)),
-        out_shape=[
-            work_shape,
-            jax.ShapeDtypeStruct((PW, 128), F32),
-            jax.ShapeDtypeStruct((8, PW), F32),
-            jax.ShapeDtypeStruct((PW, NPIV), F32),
-            jax.ShapeDtypeStruct((kid_cols, NPIV), BF16),
-            jax.ShapeDtypeStruct((NPIV, kid_cols), BF16),
-        ],
-        in_specs=[smem_spec()] * 3 + [whole_spec()] * 2,
-        out_specs=[whole_spec()] * 6,
-        scratch_shapes=[pltpu.VMEM((NPIV, NPIV), F32), pltpu.VMEM((NPIV, kid_cols), F32)],
-        compiler_params=params(),
-        cost_estimate=half_cost,
-        name="open_pivots",
-    )(place, group_of, kid_of, near, far)
-
-    begun, gathered = lax.optimization_barrier((begun, gathered))
     placed = pl.pallas_call(
         functools.partial(place_kernel, (cols, fan, tiles, slice_cols)),
         out_shape=[jax.ShapeDtypeStruct((2 * slice_cols, local_rows), BF16)] * cols,
         in_specs=[smem_spec()] * 2 + [whole_spec()],
         out_specs=[whole_spec()] * cols,
         compiler_params=params(),
-        cost_estimate=pl.CostEstimate(flops=0, bytes_accessed=8 * 2**20, transcendentals=0),
+        cost_estimate=pl.CostEstimate(flops=0, bytes_accessed=2**16, transcendentals=0),
         name="place_tiles",
     )(place, inverse_map, gathered)
-    begun, *placed = lax.optimization_barrier((begun, *placed))
+    near, far, *placed = lax.optimization_barrier((near, far, *placed))
     kid_parts = [swapped(placed[d], "col", d) for d in range(cols)]
+
+    middle = local_rows // 4
+
+    def joined(part):
+        return [
+            jnp.concatenate([value[h][:, part * middle : (part + 1) * middle] for value in (halves, others)])
+            for h in range(2)
+        ]
+
+    def last_step(value):
+        return [swapped(value[h], "col", orders[h][-1]) for h in range(2)]
+
+    early = joined(0)
+    early_far = last_step(early)
+    masks = [masks[h] + [m ^ orders[h][-1] for m in masks[h]] for h in range(2)]
+
     square = jax.ShapeDtypeStruct((PW, PW), BF16)
-    lower1, inv1_hi, inv1_lo, inv1_t_hi, inv1_t_lo, link, link_t, rest = pl.pallas_call(
-        first_kernel,
+    pivot_scratch = [
+        pltpu.VMEM((PW, PW), F32),
+        pltpu.VMEM((PW, PW), F32),
+        pltpu.VMEM((PW, 128), F32),
+        pltpu.VMEM((8, PW), F32),
+    ]
+    pivot_cost = pl.CostEstimate(flops=2 * 10**10, bytes_accessed=5 * 10**7, transcendentals=0)
+    lower1, inv1_hi, inv1_lo, inv1_t_hi, inv1_t_lo, link, link_t, rest, piv_t, piv = pl.pallas_call(
+        functools.partial(first_kernel, (cols, fan, share, held, tiles)),
         out_shape=[
             jax.ShapeDtypeStruct((2 * PW, PW), F32),
             square, square, square, square, square, square,
             jax.ShapeDtypeStruct((PW, PW), F32),
+            jax.ShapeDtypeStruct((kid_cols, NPIV), BF16),
+            jax.ShapeDtypeStruct((NPIV, kid_cols), BF16),
         ],
-        in_specs=[whole_spec()] * 4,
-        out_specs=[whole_spec()] * 8,
-        scratch_shapes=[pltpu.VMEM((PW, 2 * PW), F32)],
+        in_specs=[smem_spec()] * 3 + [whole_spec()] * 2,
+        out_specs=[whole_spec()] * 10,
+        scratch_shapes=[pltpu.VMEM((NPIV, NPIV), F32), pltpu.VMEM((NPIV, kid_cols), F32)] + pivot_scratch,
         compiler_params=params(),
-        cost_estimate=half_cost,
+        cost_estimate=pl.CostEstimate(flops=4*10**9, bytes_accessed=10**6, transcendentals=0),
         name="first_pivots",
-    )(begun, diag_col, diag_row, low_rows)
-
-    rest, *arrived = lax.optimization_barrier((rest, *halves, *others))
-    halves = [jnp.concatenate([arrived[h], arrived[2 + h]], axis=0) for h in range(2)]
-    *halves, rest, kid_parts = lax.optimization_barrier((*halves, rest, kid_parts))
-    near_kids = jnp.concatenate([part[slice_cols:] for part in kid_parts], axis=0)
-    rest, near_kids = lax.optimization_barrier((rest, near_kids))
-    far_kids = swapped(near_kids, "row", 1)
-    others = [swapped(halves[h], "col", orders[h][-1]) for h in range(2)]
-    masks = [masks[h] + [m ^ orders[h][-1] for m in masks[h]] for h in range(2)]
+    )(place, group_of, kid_of, near, far)
+    rest, *early_far = lax.optimization_barrier((rest, *early_far))
     lower2, inv2_hi, inv2_lo, inv2_t_hi, inv2_t_lo = pl.pallas_call(
         second_kernel,
         out_shape=[jax.ShapeDtypeStruct((PW, PW), F32), square, square, square, square],
         in_specs=[whole_spec()],
         out_specs=[whole_spec()] * 5,
+        scratch_shapes=pivot_scratch,
+        compiler_params=params(),
+        cost_estimate=pivot_cost,
+        name="second_pivots",
+    )(rest)
+
+    lower2, kid_parts, *others = lax.optimization_barrier((lower2, kid_parts, *others))
+    near_kids = jnp.concatenate([part[slice_cols:] for part in kid_parts], axis=0)
+    far_kids = swapped(near_kids, "row", 1)
+    late = joined(1)
+    late_far = last_step(late)
+
+    block_cols = min(1024, local_rows)
+    per_block = local_rows // block_cols
+    wide = min(512, block_cols)
+    solved_cols = pl.pallas_call(
+        functools.partial(col_kernel, (rows, fan, share, block_cols, local_rows, tiles, wide)),
+        grid=(local_cols // block_cols,),
+        out_shape=jax.ShapeDtypeStruct((NPIV, local_cols), BF16),
+        in_specs=[smem_spec()] * 3
+        + [
+            pl.BlockSpec((rows, held, block_cols), lambda j: (0, 0, j)),
+            pl.BlockSpec((kid_cols, block_cols), lambda j: (0, j % per_block)),
+            pl.BlockSpec((kid_cols, block_cols), lambda j: (0, j % per_block)),
+        ]
+        + [whole_spec()] * 6,
+        out_specs=pl.BlockSpec((NPIV, block_cols), lambda j: (0, j)),
         scratch_shapes=[
-            pltpu.VMEM((PW, 2 * PW), F32),
-            pltpu.VMEM((PW, 128), F32),
-            pltpu.VMEM((8, PW), F32),
+            pltpu.VMEM((block_cols // wide, NPIV, wide), F32),
+            pltpu.VMEM((kid_cols, block_cols), BF16),
         ],
         compiler_params=params(),
-        cost_estimate=pl.CostEstimate(flops=2 * 10**10, bytes_accessed=5 * 10**7, transcendentals=0),
-        name="second_pivots",
-    )(rest)
+        cost_estimate=pl.CostEstimate(flops=10**10, bytes_accessed=3 * 10**7, transcendentals=0),
+        name="col_factors",
+    )(
+        place, group_of, kid_of, col_strips, near_kids, far_kids,
+        piv, inv1_hi, inv1_lo, inv2_hi, inv2_lo, link,
+    )
 
     block_rows = min(256, local_rows)
-    wide = min(512, local_cols)
     depth = min(2, local_rows // block_rows // 2)
+    solved_cols, *late_far = lax.optimization_barrier((solved_cols, *late_far))
     schur_block, factor_panels = pl.pallas_call(
         functools.partial(
             schur_kernel,
-            (rows, cols, fan, share, held, slice_cols, block_rows, local_rows, local_cols, tiles, wide),
+            (cols, fan, share, held, slice_cols, block_rows, local_rows, local_cols, tiles),
             masks,
         ),
         out_shape=[
             jax.ShapeDtypeStruct((local_rows, local_cols), F32),
             jax.ShapeDtypeStruct((local_rows, NP * PW // cols), BF16),
         ],
-        in_specs=[smem_spec()] * 3 + [whole_spec()] * 14 + [any_spec()] * (8 + cols),
+        in_specs=[smem_spec()] * 3 + [whole_spec()] * 8 + [any_spec()] * (12 + cols),
         out_specs=[any_spec(), whole_spec()],
         scratch_shapes=[
             pltpu.VMEM((2 * depth, block_rows, local_cols), F32),
             pltpu.VMEM((2 * depth, block_rows, local_cols), F32),
-            pltpu.VMEM((rows, held, local_cols), BF16),
             pltpu.VMEM((kid_cols, local_cols), BF16),
             pltpu.VMEM((kid_cols, local_rows), BF16),
             pltpu.VMEM((cols, local_rows, fan * held), F32),
             pltpu.VMEM((NPIV, local_cols), BF16),
-            pltpu.VMEM((2, NPIV, wide), F32),
             pltpu.VMEM((block_rows, NPIV), F32),
             pltpu.VMEM((block_rows, NPIV), F32),
             pltpu.VMEM((block_rows, kid_cols), BF16),
             pltpu.VMEM((block_rows, kid_cols), BF16),
             pltpu.SemaphoreType.DMA((2 * depth,)),
             pltpu.SemaphoreType.DMA((2 * depth,)),
-            pltpu.SemaphoreType.DMA((local_cols // wide,)),
+            pltpu.SemaphoreType.DMA,
             pltpu.SemaphoreType.DMA((fan,)),
             pltpu.SemaphoreType.DMA((cols,)),
-            pltpu.SemaphoreType.DMA((2 * cols,)),
+            pltpu.SemaphoreType.DMA((4 * cols,)),
         ],
         compiler_params=params(),
         cost_estimate=pl.CostEstimate(flops=3 * 10**10, bytes_accessed=9 * 10**7, transcendentals=0),
         name="schur_update",
     )(
-        place, group_of, kid_of,
-        piv, piv_t, lower1, lower2, inv1_hi, inv1_lo, inv2_hi, inv2_lo, link,
+        place, group_of, kid_of, piv_t, lower1, lower2,
         inv1_t_hi, inv1_t_lo, inv2_t_hi, inv2_t_lo, link_t,
-        front_entries, col_strips, near_kids, far_kids, *kid_parts,
-        halves[0], others[0], halves[1], others[1],
+        front_entries, solved_cols, near_kids, far_kids, *kid_parts,
+        early[0], early_far[0], late[0], late_far[0], early[1], early_far[1], late[1], late_far[1],
     )
     return (factor_panels, schur_block)
 

time: 152 us -> 147 us (0.967)
  waiting for transfers between devices: 27.1 us -> 19.8 us
  starting transfers between devices: 18.3 us -> 20.4 us
    ppermute x15 -> x17, waiting for transfers between devices: 26.3 us -> 19.1 us  [swapped(): lax.ppermute(value, axis, [(i, i ^ mask) for i in range(lax.axis_size(axi...]
    pallas_call x1, Pallas kernels: 16.6 us -> 13.7 us  [local(): pl.pallas_call(second_kernel, out_shape=[jax.ShapeDtypeStruct((PW, PW), F...]
    pallas_call x3, Pallas kernels: 55.8 us -> 58.6 us  [the longest x1 33.4 us: local(): pl.pallas_call(functools.partial(schur_kernel, (cols, fan, share, held, s...]
    ppermute x15 -> x17, starting transfers between devices: 18.2 us -> 20.3 us  [swapped(): lax.ppermute(value, axis, [(i, i ^ mask) for i in range(lax.axis_size(axi...]
  transfers between devices with their start and end apart: 17 -> 19, of which waited for: 7 -> 7; matrix products, arithmetic and copies ran while one was open for 9% -> 10% of each run, Pallas kernels for 27% -> 29%
where the time goes in v3:
time: 147 us
  Pallas kernels  76.3 us (52%)
  starting transfers between devices  20.4 us (14%)
  waiting for transfers between devices  19.8 us (13%)
  between operations  14.4 us (10%)
  local copies, waits for them, and re-layouts  10.7 us (7%)
  other arithmetic  4.98 us (3%)
    pallas_call x1, Pallas kernels, local(): pl.pallas_call(functools.partial(schur_kernel, (cols, fan, share, held, s...  33.4 us
    ppermute x17, starting transfers between devices, swapped(): lax.ppermute(value, axis, [(i, i ^ mask) for i in range(lax.axis_size(axi...  20.3 us
    ppermute x17, waiting for transfers between devices, swapped(): lax.ppermute(value, axis, [(i, i ^ mask) for i in range(lax.axis_size(axi...  19.1 us
    pallas_call x1, Pallas kernels, local(): pl.pallas_call(functools.partial(first_kernel, (cols, fan, share, held, t...  16.1 us
    pallas_call x1, Pallas kernels, local(): pl.pallas_call(second_kernel, out_shape=[jax.ShapeDtypeStruct((PW, PW), F...  13.7 us
    pallas_call x1, Pallas kernels, local(): pl.pallas_call(functools.partial(col_kernel, (rows, fan, share, block_col...  9.13 us
    pallas_call x1, Pallas kernels, local(): pl.pallas_call(functools.partial(place_kernel, (cols, fan, tiles, slice_c...  3.98 us
  transfers between devices with their start and end apart: 19, of which 7 were waited for; matrix products, arithmetic and copies ran while one was open for 10% of the time, Pallas kernels for 29%

profile of v3, /device:TPU:0, one launch (start us, length us, event | category | flops | bytes accessed | tf_op | source)
XLA Modules:
  0.0 146.5 jit_solution(7495108466824928560)
XLA Ops:
  7.2 0.7 all-gather.5.cloned.1.call-update
  8.0 1.0 copy.6
  8.9 0.7 broadcast_compare_fusion
  10.1 0.9 fusion.1
  11.1 5.1 %collective-permute-start.2 = (f32[128,128]{1,0:T(8,128)S(1)}, f32[128,128]{1,0:T(8,128)S(1)}, u32[]{:S(2)}, u32[]{:S(2)}) collective-permute-start(f32[128,128]{1,0:T(8,128)S(1)} %maximum_maximum_fusion), channel_id=1, source_target_pairs={{0,24},{4,28},{8,16},{12,20},{16,8},{20,12},{24,0},{28,4},{1,25},{... | collective-permute-start | bytes 196616 | tf_op jit(solution)/shard_map/ppermute | solution.py:41
  16.2 0.6 collective-permute-start
  16.9 2.9 %fusion.2 = (f32[2048,32]{1,0:T(8,128)S(1)}, f32[2048,32]{1,0:T(8,128)S(1)}, f32[2048,32]{1,0:T(8,128)S(1)}, f32[2048,32]{1,0:T(8,128)S(1)}) fusion(f32[2048,4096]{1,0:T(8,128)} %refs_0_.1), kind=kLoop, calls=%fused_computation.30 | loop fusion | bytes 2097152 | tf_op jit(solution)/shard_map/slice | solution.py:495
  19.8 0.9 pad_maximum_fusion
  20.7 2.1 %slice.206 = bf16[64,4096]{1,0:T(8,128)(2,1)} slice(f32[2048,4096]{1,0:T(8,128)} %refs_0_.1), slice={[0:64], [0:4096]} | slice | bytes 1048576 | tf_op jit(solution)/shard_map/slice | solution.py:503
  23.3 1.7 %collective-permute-start.4 = (f32[4,96,128]{2,1,0:T(8,128)S(1)}, f32[4,96,128]{2,1,0:T(8,128)S(1)}, u32[]{:S(2)}, u32[]{:S(2)}) collective-permute-start(f32[4,96,128]{2,1,0:T(8,128)S(1)} %get-tuple-element.111), channel_id=1, source_target_pairs={{0,2},{1,3},{2,0},{3,1},{4,6},{5,7},{6,4},{7,5},{8,10},{9,11},{10,... | collective-permute-start | bytes 589832 | tf_op jit(solution)/shard_map/ppermute | solution.py:41
  25.1 1.5 %collective-permute-start.3 = (f32[4,96,128]{2,1,0:T(8,128)S(1)}, f32[4,96,128]{2,1,0:T(8,128)S(1)}, u32[]{:S(2)}, u32[]{:S(2)}) collective-permute-start(f32[4,96,128]{2,1,0:T(8,128)S(1)} %get-tuple-element.111), channel_id=1, source_target_pairs={{0,1},{1,0},{2,3},{3,2},{4,5},{5,4},{6,7},{7,6},{8,9},{9,8},{10,11... | collective-permute-start | bytes 589832 | tf_op jit(solution)/shard_map/ppermute | solution.py:41
  27.0 1.7 %collective-permute-start.7 = (f32[1,1024,128]{2,1,0:T(8,128)S(1)}, f32[1,1024,128]{2,1,0:T(8,128)S(1)}, u32[]{:S(2)}, u32[]{:S(2)}) collective-permute-start(f32[1,1024,128]{2,1,0:T(8,128)S(1)} %get-tuple-element.105), channel_id=1, source_target_pairs={{0,1},{1,0},{2,3},{3,2},{4,5},{5,4},{6,7},{7,6},{8,9},{9,8},{10,11... | collective-permute-start | bytes 1572872 | tf_op jit(solution)/shard_map/ppermute | solution.py:41
  28.7 1.5 %collective-permute-start.9 = (f32[1,1024,128]{2,1,0:T(8,128)S(1)}, f32[1,1024,128]{2,1,0:T(8,128)S(1)}, u32[]{:S(2)}, u32[]{:S(2)}) collective-permute-start(f32[1,1024,128]{2,1,0:T(8,128)S(1)} %get-tuple-element.104), channel_id=1, source_target_pairs={{0,2},{1,3},{2,0},{3,1},{4,6},{5,7},{6,4},{7,5},{8,10},{9,11},{10,... | collective-permute-start | bytes 1572872 | tf_op jit(solution)/shard_map/ppermute | solution.py:41
  30.3 1.0 collective-permute-done.4
  31.3 1.6 %collective-permute-done.3 = f32[4,96,128]{2,1,0:T(8,128)S(1)} collective-permute-done((f32[4,96,128]{2,1,0:T(8,128)S(1)}, f32[4,96,128]{2,1,0:T(8,128)S(1)}, u32[]{:S(2)}, u32[]{:S(2)}) %collective-permute-start.3) | collective-permute-done | bytes 196640 | tf_op jit(solution)/shard_map/ppermute | solution.py:41
  32.9 4.0 %collective-permute-done.5 = f32[4,96,128]{2,1,0:T(8,128)S(1)} collective-permute-done((f32[4,96,128]{2,1,0:T(8,128)S(1)}, f32[4,96,128]{2,1,0:T(8,128)S(1)}, u32[]{:S(2)}, u32[]{:S(2)}) %collective-permute-start.5) | collective-permute-done | bytes 196640 | tf_op jit(solution)/shard_map/ppermute | solution.py:41
  37.2 9.0 %collective-permute-done.7 = f32[1,1024,128]{2,1,0:T(8,128)S(1)} collective-permute-done((f32[1,1024,128]{2,1,0:T(8,128)S(1)}, f32[1,1024,128]{2,1,0:T(8,128)S(1)}, u32[]{:S(2)}, u32[]{:S(2)}) %collective-permute-start.7) | collective-permute-done | bytes 524320 | tf_op jit(solution)/shard_map/ppermute | solution.py:41
  46.2 0.7 collective-permute-start.8
  47.0 0.9 pad_maximum_fusion.4.refs_12_
  47.8 1.4 collective-permute-start.10
  49.8 0.7 convert_element_type.19.group_of
  51.1 4.0 %place_tiles.1 = (bf16[128,2048]{1,0:T(8,128)(2,1)}, bf16[128,2048]{1,0:T(8,128)(2,1)}, bf16[128,2048]{1,0:T(8,128)(2,1)}, bf16[128,2048]{1,0:T(8,128)(2,1)}) custom-call(s32[2]{0:T(128)} %pad_add_fusion.place, s32[128]{0:T(128)} %copy-done.9, bf16[8,64,2048]{2,1,0:T(8,128)(2,1)} %bitcast.24), custom_call_target="tpu_custom_call" | custom-call | bytes 65536 | tf_op jit(solution)/shard_map/place_tiles/pallas_call | solution.py:536
  55.7 1.4 collective-permute-start.12
  57.1 1.5 %collective-permute-start.13 = (bf16[128,2048]{1,0:T(8,128)(2,1)}, bf16[128,2048]{1,0:T(8,128)(2,1)}, u32[]{:S(2)}, u32[]{:S(2)}) collective-permute-start(bf16[128,2048]{1,0:T(8,128)(2,1)} %get-tuple-element.67), channel_id=1, source_target_pairs={{0,3},{1,2},{2,1},{3,0},{4,7},{5,6},{6,5},{7,4},{8,11},{9,10},{10,... | collective-permute-start | bytes 1572872 | tf_op jit(solution)/shard_map/ppermute | solution.py:41
  58.6 16.1 %first_pivots.1 = (f32[512,256]{1,0:T(8,128)}, bf16[256,256]{1,0:T(8,128)(2,1)}, bf16[256,256]{1,0:T(8,128)(2,1)}, bf16[256,256]{1,0:T(8,128)(2,1)}, bf16[256,25...) custom-call(s32[2]{0:T(128)} %pad_add_fusion.place, ...), custom_call_target="tpu_custom_call" | custom-call | flops 4000000000 | bytes 1000000 | tf_op jit(solution)/shard_map/first_pivots/pallas_call | solution.py:571
  74.7 13.7 %second_pivots.1 = (f32[256,256]{1,0:T(8,128)}, bf16[256,256]{1,0:T(8,128)(2,1)}, bf16[256,256]{1,0:T(8,128)(2,1)}, bf16[256,256]{1,0:T(8,128)(2,1)}, bf16[256,256]{1,0:T(8,128)(2,1)}) custom-call(f32[256,256]{1,0:T(8,128)} %get-tuple-element.62.rest), custom_call_target="tpu_custom_call" | custom-call | flops 20000000000 | bytes 50000000 | tf_op jit(solution)/shard_map/second_pivots/pallas_call | solution.py:588
  88.6 0.7 copy-done.6
  89.4 1.0 slice.172
  91.4 1.5 collective-permute-start.15
  93.4 9.1 %col_factors.1.refs_1_ = bf16[512,4096]{1,0:T(8,128)(2,1)} custom-call(s32[2]{0:T(128)} %pad_add_fusion.place, f32[128]{0:T(128)} %convert_element_type.19.group_of, f32[128]{0:T(128)} %compare_convert_fusion.kid_of, bf16[8,64,4096]{2,1,0:T(8,128)(2,1)} %bitcast.31, bf16[256,2048]{1,0:T(8,128)(2,1)} %copy-done, ...), custom_call_target="tpu_custom_call" | custom-call | flops 10000000000 | bytes 30000000 | tf_op jit(solution)/shard_map/col_factors/pallas_call | solution.py:608
  102.5 2.6 %collective-permute-done.16.refs_15_ = f32[2,512,128]{2,1,0:T(8,128)S(1)} collective-permute-done((f32[2,512,128]{2,1,0:T(8,128)S(1)}, f32[2,512,128]{2,1,0:T(8,128)S(1)}, u32[]{:S(2)}, u32[]{:S(2)}) %collective-permute-start.16) | collective-permute-done | bytes 524320 | tf_op jit(solution)/shard_map/ppermute | solution.py:41
  106.3 33.4 %schur_update.1 = (f32[2048,4096]{1,0:T(8,128)}, bf16[2048,128]{1,0:T(8,128)(2,1)}) custom-call(s32[2]{0:T(128)} %pad_add_fusion.place, f32[128]{0:T(128)} %convert_element_type.19.group_of, f32[128]{0:T(128)} %compare_convert_fusion.kid_of, bf16[256,512]{1,0:T(8,128)(2,1)} %get-tuple-element.58.piv_t, f32[512,256]{1,0:T(8,128)} %get-tuple-element.59.lower1, ...), custom_call_target="tpu_custom_call" | custom-call | flops 30000001024 | bytes 90000000 | tf_op jit(solution)/shard_map/schur_update/pallas_call | solution.py:635
  (83 shorter events, 6.6 us)
Async XLA Ops:
  7.2 44.0 %all-gather.5.cloned.1.call-start = ((), (), s32[]{:S(2)}) async-start(), calls=%async_computation | async-start | bytes 2359296 | tf_op jit(solution)/shard_map/all_gather | solution.py:501
  7.9 85.5 %all-gather.7.cloned.1.call-start = ((), (), s32[]{:S(2)}) async-start(), calls=%async_computation.1 | async-start | bytes 4718592 | tf_op jit(solution)/shard_map/all_gather | solution.py:505
  11.1 11.7 %collective-permute-start.2 = (f32[128,128]{1,0:T(8,128)S(1)}, f32[128,128]{1,0:T(8,128)S(1)}, u32[]{:S(2)}, u32[]{:S(2)}) collective-permute-start(f32[128,128]{1,0:T(8,128)S(1)} %maximum_maximum_fusion), channel_id=1, source_target_pairs={{0,24},{4,28},{8,16},{12,20},{16,8},{20,12},{24,0},{28,4},{1,25},{... | collective-permute-start | bytes 196616 | tf_op jit(solution)/shard_map/ppermute | solution.py:41
  16.2 6.5 %collective-permute-start.1 = (f32[128,128]{1,0:T(8,128)S(1)}, f32[128,128]{1,0:T(8,128)S(1)}, u32[]{:S(2)}, u32[]{:S(2)}) collective-permute-start(f32[128,128]{1,0:T(8,128)S(1)} %maximum_maximum_fusion), channel_id=1, source_target_pairs={{0,16},{4,20},{8,24},{12,28},{16,0},{20,4},{24,8},{28,12},{1,17},{... | collective-permute-start | bytes 196616 | tf_op jit(solution)/shard_map/ppermute | solution.py:41
  16.2 6.5 %collective-permute-start = (f32[128,128]{1,0:T(8,128)S(1)}, f32[128,128]{1,0:T(8,128)S(1)}, u32[]{:S(2)}, u32[]{:S(2)}) collective-permute-start(f32[128,128]{1,0:T(8,128)S(1)} %maximum_maximum_fusion), channel_id=1, source_target_pairs={{0,8},{4,12},{8,0},{12,4},{16,24},{20,28},{24,16},{28,20},{1,9},{5... | collective-permute-start | bytes 196616 | tf_op jit(solution)/shard_map/ppermute | solution.py:41
  22.8 7.4 %copy-start.8 = (s32[128]{0:T(128)S(1)}, s32[128]{0:T(128)}, u32[]{:S(2)}) copy-start(s32[128]{0:T(128)} %param.7) | copy-start | bytes 1540
  23.3 8.0 %collective-permute-start.4 = (f32[4,96,128]{2,1,0:T(8,128)S(1)}, f32[4,96,128]{2,1,0:T(8,128)S(1)}, u32[]{:S(2)}, u32[]{:S(2)}) collective-permute-start(f32[4,96,128]{2,1,0:T(8,128)S(1)} %get-tuple-element.111), channel_id=1, source_target_pairs={{0,2},{1,3},{2,0},{3,1},{4,6},{5,7},{6,4},{7,5},{8,10},{9,11},{10,... | collective-permute-start | bytes 589832 | tf_op jit(solution)/shard_map/ppermute | solution.py:41
  25.1 7.8 %collective-permute-start.3 = (f32[4,96,128]{2,1,0:T(8,128)S(1)}, f32[4,96,128]{2,1,0:T(8,128)S(1)}, u32[]{:S(2)}, u32[]{:S(2)}) collective-permute-start(f32[4,96,128]{2,1,0:T(8,128)S(1)} %get-tuple-element.111), channel_id=1, source_target_pairs={{0,1},{1,0},{2,3},{3,2},{4,5},{5,4},{6,7},{7,6},{8,9},{9,8},{10,11... | collective-permute-start | bytes 589832 | tf_op jit(solution)/shard_map/ppermute | solution.py:41
  26.6 10.4 %collective-permute-start.5 = (f32[4,96,128]{2,1,0:T(8,128)S(1)}, f32[4,96,128]{2,1,0:T(8,128)S(1)}, u32[]{:S(2)}, u32[]{:S(2)}) collective-permute-start(f32[4,96,128]{2,1,0:T(8,128)S(1)} %get-tuple-element.111), channel_id=1, source_target_pairs={{0,3},{1,2},{2,1},{3,0},{4,7},{5,6},{6,5},{7,4},{8,11},{9,10},{10,... | collective-permute-start | bytes 589832 | tf_op jit(solution)/shard_map/ppermute | solution.py:41
  27.0 19.2 %collective-permute-start.7 = (f32[1,1024,128]{2,1,0:T(8,128)S(1)}, f32[1,1024,128]{2,1,0:T(8,128)S(1)}, u32[]{:S(2)}, u32[]{:S(2)}) collective-permute-start(f32[1,1024,128]{2,1,0:T(8,128)S(1)} %get-tuple-element.105), channel_id=1, source_target_pairs={{0,1},{1,0},{2,3},{3,2},{4,5},{5,4},{6,7},{7,6},{8,9},{9,8},{10,11... | collective-permute-start | bytes 1572872 | tf_op jit(solution)/shard_map/ppermute | solution.py:41
  28.7 18.3 %collective-permute-start.9 = (f32[1,1024,128]{2,1,0:T(8,128)S(1)}, f32[1,1024,128]{2,1,0:T(8,128)S(1)}, u32[]{:S(2)}, u32[]{:S(2)}) collective-permute-start(f32[1,1024,128]{2,1,0:T(8,128)S(1)} %get-tuple-element.104), channel_id=1, source_target_pairs={{0,2},{1,3},{2,0},{3,1},{4,6},{5,7},{6,4},{7,5},{8,10},{9,11},{10,... | collective-permute-start | bytes 1572872 | tf_op jit(solution)/shard_map/ppermute | solution.py:41
  30.3 18.9 %copy-start.9 = (s32[128]{0:T(128)}, s32[128]{0:T(128)S(1)}, u32[]{:S(2)}) copy-start(s32[128]{0:T(128)S(1)} %select_reduce_fusion.inverse_map) | copy-start | bytes 1540
  37.0 10.0 %copy-start.1 = (f32[4,4,96,128]{3,2,1,0:T(8,128)}, f32[4,4,96,128]{3,2,1,0:T(8,128)S(1)}, u32[]{:S(2)}) copy-start(f32[4,4,96,128]{3,2,1,0:T(8,128)S(1)} %pad_maximum_fusion.2.near) | copy-start | bytes 2359300
  37.0 18.1 %collective-permute-start.6 = (f32[4,4,96,128]{3,2,1,0:T(8,128)S(1)}, f32[4,4,96,128]{3,2,1,0:T(8,128)}, u32[]{:S(2)}, u32[]{:S(2)}) collective-permute-start(f32[4,4,96,128]{3,2,1,0:T(8,128)S(1)} %pad_maximum_fusion.2.near), channel_id=1, source_target_pairs={{0,4},{4,0},{8,12},{12,8},{16,20},{20,16},{24,28},{28,24},{1,5},{5... | collective-permute-start | bytes 2359304 | tf_op jit(solution)/shard_map/ppermute | solution.py:41
  37.2 12.6 %copy-start.12 = (s32[32]{0:T(128)S(1)}, s32[32]{0:T(128)}, u32[]{:S(2)}) copy-start(s32[32]{0:T(128)} %param.5) | copy-start | bytes 388
  46.2 28.5 %copy-start.2 = (f32[2,512,128]{2,1,0:T(8,128)}, f32[2,512,128]{2,1,0:T(8,128)S(1)}, u32[]{:S(2)}) copy-start(f32[2,512,128]{2,1,0:T(8,128)S(1)} %pad_maximum_fusion.3.refs_8_) | copy-start | bytes 1572868
  46.2 28.5 %collective-permute-start.8 = (f32[2,512,128]{2,1,0:T(8,128)S(1)}, f32[2,512,128]{2,1,0:T(8,128)}, u32[]{:S(2)}, u32[]{:S(2)}) collective-permute-start(f32[2,512,128]{2,1,0:T(8,128)S(1)} %pad_maximum_fusion.3.refs_8_), channel_id=1, source_target_pairs={{0,2},{1,3},{2,0},{3,1},{4,6},{5,7},{6,4},{7,5},{8,10},{9,11},{10,... | collective-permute-start | bytes 1572872 | tf_op jit(solution)/shard_map/ppermute | solution.py:41
  47.8 26.9 %collective-permute-start.10 = (f32[2,512,128]{2,1,0:T(8,128)}, f32[2,512,128]{2,1,0:T(8,128)}, u32[]{:S(2)}, u32[]{:S(2)}) collective-permute-start(f32[2,512,128]{2,1,0:T(8,128)} %pad_maximum_fusion.4.refs_12_), channel_id=1, source_target_pairs={{0,1},{1,0},{2,3},{3,2},{4,5},{5,4},{6,7},{7,6},{8,9},{9,8},{10,11... | collective-permute-start | bytes 1572872 | tf_op jit(solution)/shard_map/ppermute | solution.py:41
  55.1 33.3 %collective-permute-start.11 = (bf16[128,2048]{1,0:T(8,128)(2,1)}, bf16[128,2048]{1,0:T(8,128)(2,1)S(1)}, u32[]{:S(2)}, u32[]{:S(2)}) collective-permute-start(bf16[128,2048]{1,0:T(8,128)(2,1)} %get-tuple-element.65), channel_id=1, source_target_pairs={{0,1},{1,0},{2,3},{3,2},{4,5},{5,4},{6,7},{7,6},{8,9},{9,8},{10,11... | collective-permute-start | bytes 1572872 | tf_op jit(solution)/shard_map/ppermute | solution.py:41
  55.7 32.8 %collective-permute-start.12 = (bf16[128,2048]{1,0:T(8,128)(2,1)}, bf16[128,2048]{1,0:T(8,128)(2,1)S(1)}, u32[]{:S(2)}, u32[]{:S(2)}) collective-permute-start(bf16[128,2048]{1,0:T(8,128)(2,1)} %get-tuple-element.66), channel_id=1, source_target_pairs={{0,2},{1,3},{2,0},{3,1},{4,6},{5,7},{6,4},{7,5},{8,10},{9,11},{10,... | collective-permute-start | bytes 1572872 | tf_op jit(solution)/shard_map/ppermute | solution.py:41
  57.1 31.4 %collective-permute-start.13 = (bf16[128,2048]{1,0:T(8,128)(2,1)}, bf16[128,2048]{1,0:T(8,128)(2,1)}, u32[]{:S(2)}, u32[]{:S(2)}) collective-permute-start(bf16[128,2048]{1,0:T(8,128)(2,1)} %get-tuple-element.67), channel_id=1, source_target_pairs={{0,3},{1,2},{2,1},{3,0},{4,7},{5,6},{6,5},{7,4},{8,11},{9,10},{10,... | collective-permute-start | bytes 1572872 | tf_op jit(solution)/shard_map/ppermute | solution.py:41
  74.7 13.8 %copy-start.5 = (bf16[128,2048]{1,0:T(8,128)(2,1)S(1)}, bf16[128,2048]{1,0:T(8,128)(2,1)}, u32[]{:S(2)}) copy-start(bf16[128,2048]{1,0:T(8,128)(2,1)} %get-tuple-element.75.refs_4_) | copy-start | bytes 1572868
  88.4 0.8 copy-start.6
  88.4 1.0 copy-start.7
  90.5 2.9 %copy-start = (bf16[256,2048]{1,0:T(8,128)(2,1)}, bf16[256,2048]{1,0:T(8,128)(2,1)S(1)}, u32[]{:S(2)}) copy-start(bf16[256,2048]{1,0:T(8,128)(2,1)S(1)} %pad_maximum_fusion.1.near_kids.refs_2_) | copy-start | bytes 3145732
  90.5 2.9 %collective-permute-start.14 = (bf16[256,2048]{1,0:T(8,128)(2,1)S(1)}, bf16[256,2048]{1,0:T(8,128)(2,1)}, u32[]{:S(2)}, u32[]{:S(2)}) collective-permute-start(bf16[256,2048]{1,0:T(8,128)(2,1)S(1)} %pad_maximum_fusion.1.near_kids.refs_2_), channel_id=1, source_target_pairs={{0,4},{4,0},{8,12},{12,8},{16,20},{20,16},{24,28},{28,24},{1,5},{5... | collective-permute-start | bytes 3145736 | tf_op jit(solution)/shard_map/ppermute | solution.py:41
  90.7 11.8 %copy-start.3 = (f32[2,512,128]{2,1,0:T(8,128)}, f32[2,512,128]{2,1,0:T(8,128)S(1)}, u32[]{:S(2)}) copy-start(f32[2,512,128]{2,1,0:T(8,128)S(1)} %pad_maximum_fusion.6.refs_14_) | copy-start | bytes 1572868
  90.7 14.4 %collective-permute-start.16 = (f32[2,512,128]{2,1,0:T(8,128)S(1)}, f32[2,512,128]{2,1,0:T(8,128)S(1)}, u32[]{:S(2)}, u32[]{:S(2)}) collective-permute-start(f32[2,512,128]{2,1,0:T(8,128)S(1)} %pad_maximum_fusion.6.refs_14_), channel_id=1, source_target_pairs={{0,1},{1,0},{2,3},{3,2},{4,5},{5,4},{6,7},{7,6},{8,9},{9,8},{10,11... | collective-permute-start | bytes 1572872 | tf_op jit(solution)/shard_map/ppermute | solution.py:41
  91.4 11.1 %copy-start.4 = (f32[2,512,128]{2,1,0:T(8,128)}, f32[2,512,128]{2,1,0:T(8,128)S(1)}, u32[]{:S(2)}) copy-start(f32[2,512,128]{2,1,0:T(8,128)S(1)} %pad_maximum_fusion.5.refs_10_) | copy-start | bytes 1572868
  91.4 14.1 %collective-permute-start.15 = (f32[2,512,128]{2,1,0:T(8,128)S(1)}, f32[2,512,128]{2,1,0:T(8,128)S(1)}, u32[]{:S(2)}, u32[]{:S(2)}) collective-permute-start(f32[2,512,128]{2,1,0:T(8,128)S(1)} %pad_maximum_fusion.5.refs_10_), channel_id=1, source_target_pairs={{0,2},{1,3},{2,0},{3,1},{4,6},{5,7},{6,4},{7,5},{8,10},{9,11},{10,... | collective-permute-start | bytes 1572872 | tf_op jit(solution)/shard_map/ppermute | solution.py:41
  105.1 0.8 copy-start.10
  105.5 0.8 copy-start.11
Sparse Core Ops, SparseCore 0:
  9.6 31.7 all-gather.4
  43.6 46.7 all-gather.6
